TPU v7x, 512 devices: a whole 4x8x8 slice. The times are simulated.
512 devices in a mesh: day: 16 (over y, core), bl: 32 (over z, x).
Axes of the slice: x: 4, y: 8, z: 8, core: 2. Of those that a mesh axis runs over, the one named last changes fastest.
Arguments:
- visibility: bfloat16 [16, 16, 2, 2048, 512], P('day', None, None, 'bl'), may hold values from -6 to 6
- day_weight: float32 [16, 2048, 512], P('day', 'bl'), may hold values from 0.2 to 5
- day_offset: int32 [16], replicated, may hold values from 0 to 16, as said below
- pair_index: int32 [2048], replicated, may hold values from 0 to 3, as said below
- sep_index: int32 [2048], replicated, may hold values from 0 to 511, as said below
Outputs:
- skymap: float32 [512, 32, 4, 512], P('bl', 'day')
Inputs may be any that keep to these rules, and one draw needn't show every extreme that they name: Each day's samples cover 32 bins day_offset to day_offset + 15; every 32 bin of the window is covered by some day; some day starts at 0 and some at 16. `pair_index`: each pair of cylinder separation and north-south separation is named by exactly one stacked baseline. `sep_index`: each pair of cylinder separation and north-south separation is named by exactly one stacked baseline.
All inputs are finite; a program needn't handle non-finite values.
Results may differ from a plain program's by a relative error of at most 0.0032.
Values may be sent and summed in bfloat16 or wider, within the bound.
No kernel may reach another device: no remote copies, remote signals or barrier semaphores. Data moves between devices by JAX's collectives and lax.ppermute only.
A program may use at most 64 MiB of HBM per device.

v0:
```python
import jax
import jax.numpy as jnp
from jax import lax
from jax.sharding import PartitionSpec as P

FREQ = 512
PAIRS = 4
NSEP = 512
PIXELS = 512
RA_DEV = 2
BASES = 2048


phase_scale = 2.0 * 3.141592653589793 * 0.3048 / 299.792458


def ns_table(freq_at):
    freq_value = 800.0 - 400.0 * (freq_at + 0.5) / FREQ
    sine_dir = -1.0 + 2.0 * (jnp.arange(PIXELS).astype(jnp.float32) + 0.5) / PIXELS
    separation = jnp.arange(NSEP).astype(jnp.float32) - NSEP // 2
    factor = phase_scale * freq_value
    phase = factor[:, None, None] * separation[None, :, None] * sine_dir[None, None, :]
    return jnp.concatenate(
        [jnp.cos(phase).astype(jnp.bfloat16), (-jnp.sin(phase)).astype(jnp.bfloat16)], axis=1
    )


def local(visibility, day_weight, day_offset, pair_index, sep_index):
    day_count = lax.axis_size("day")
    my_day = lax.axis_index("day")
    my_band = lax.axis_index("bl")
    local_days = visibility.shape[0]
    sample_len = visibility.shape[1]
    base_local = visibility.shape[3]
    ra_total = RA_DEV * day_count
    all_weights = lax.all_gather(day_weight, "day", axis=0, tiled=True)
    ra_rows = my_day * RA_DEV + jnp.arange(RA_DEV)
    shifted = ra_rows[None, :] - day_offset[:, None]
    valid = ((shifted >= 0) & (shifted < sample_len)).astype(jnp.float32)
    total = jnp.einsum("dr,dbf->rbf", valid, all_weights, precision=lax.Precision.HIGHEST)
    local_offsets = lax.dynamic_slice_in_dim(day_offset, my_day * local_days, local_days)

    def place_day(one_day, start):
        zero_at = jnp.zeros((), jnp.int32)
        empty = jnp.zeros((ra_total, 2, base_local, FREQ), jnp.bfloat16)
        return lax.dynamic_update_slice(empty, one_day, (start, zero_at, zero_at, zero_at))

    placed = jax.vmap(place_day)(visibility, local_offsets)
    outgoing = placed.reshape(local_days, day_count, RA_DEV, 2, base_local, FREQ)
    received = lax.all_to_all(outgoing, "day", split_axis=1, concat_axis=0, tiled=True)
    received = received.reshape(local_days * day_count, RA_DEV, 2, base_local, FREQ)

    def add_day(day_at, running):
        one_day = lax.dynamic_index_in_dim(received, day_at, 0, keepdims=False)
        weight_now = lax.dynamic_index_in_dim(all_weights, day_at, 0, keepdims=False)
        return running + one_day.astype(jnp.float32) * weight_now[None, None]

    summed = lax.fori_loop(
        0, local_days * day_count, add_day, jnp.zeros((RA_DEV, 2, base_local, FREQ), jnp.float32)
    )
    stack = (summed / total[:, None]).astype(jnp.bfloat16)
    cell_key = pair_index * NSEP + sep_index
    onehot = (cell_key[:, None] == jnp.arange(PAIRS * NSEP)[None, :]).astype(jnp.bfloat16)
    onehot = onehot.reshape(BASES, PAIRS, NSEP)
    band_width = FREQ // lax.axis_size("bl")
    freq_at = (my_band * band_width + jnp.arange(band_width)).astype(jnp.float32)
    table = ns_table(freq_at)
    block = lax.all_to_all(stack, "bl", split_axis=3, concat_axis=2, tiled=True)
    items = block.shape[0]
    grid = jnp.einsum("kxbf,bcn->fkcxn", block, onehot, preferred_element_type=jnp.float32).astype(
        jnp.bfloat16
    )
    grid = grid.reshape(band_width, items * PAIRS, 2 * NSEP)
    result = jnp.einsum("fmq,fqp->fmp", grid, table, preferred_element_type=jnp.float32)
    return result.reshape(band_width, items, PAIRS, PIXELS)


def solution(mesh):
    return jax.shard_map(
        local,
        mesh=mesh,
        in_specs=(P("day", None, None, "bl", None), P("day", "bl", None), P(), P(), P()),
        out_specs=P("bl", "day", None, None),
        check_vma=False,
    )
```

profile of v0, /device:TPU:1, one launch (start us, length us, event | category | flops | bytes accessed | tf_op | source)
XLA Modules:
  0.0 264.3 jit_solution(4437805472720334983)
XLA Ops:
  6.5 1.2 dynamic_slice.19
  9.7 0.7 fusion.26
  10.5 0.7 fusion.34
  11.1 2.5 concatenate.25
  13.7 1.3 and_reduce_fusion
  15.0 0.5 broadcast_in_dim.8
  15.5 3.3 %select_dynamic-update-slice_fusion = bf16[1,32,2,64,512]{4,3,2,1,0:T(8,128)(2,1)S(1)} fusion(bf16[1,32,2,64,512]{4,3,2,1,0:T(8,128)(2,1)S(1)} %broadcast_in_dim.8, s32[]{:T(128)} %bitcast.7, bf16[1,16,2,64,512]{4,3,2,1,0:T(8,128)(2,1)} %param.9, pred[]{:T(512)} %and_reduce_fusion), kind=kLoop, calls=%fused_computation.19 | loop fusion | flops 1048576 | bytes 4194309 | tf_op jit(solution)/shard_map/vmap(vmap())/scatter | solution.py:46
  18.8 2.0 copy-done
  20.8 11.2 %all-to-all-start = ((bf16[1,16,2,2,64,512]{5,4,3,2,0,1:T(8,128)(2,1)}), bf16[1,16,2,2,64,512]{5,4,3,2,0,1:T(8,128)(2,1)}, u32[]{:S(2)}, u32[]{:S(2)}) async-start(bf16[1,16,2,2,64,512]{5,4,3,2,0,1:T(8,128)(2,1)} %bitcast.46), calls=%async_computation | async-start | bytes 8388608 | tf_op jit(solution)/shard_map/all_to_all | solution.py:50
  31.9 0.0 all-gather.2.cloned.1.call-start
  32.0 0.7 all-gather.2.cloned.1.call-update
  32.7 0.1 broadcast_multiply_fusion
  32.8 70.6 %all-gather.2.cloned.1.call-done = f32[16,64,512]{2,1,0:T(8,128)} async-done(((f32[1,64,512]{2,1,0:T(8,128)}), f32[16,64,512]{2,1,0:T(8,128)}) %all-gather.2.cloned.1.call-update) | async-done | bytes 2097168 | tf_op jit(solution)/shard_map/all_gather | solution.py:36
  103.4 3.5 %fusion.13 = f32[2,64,512]{2,0,1:T(2,128)S(1)} fusion(f32[16,64,512]{2,1,0:T(8,128)} %all-gather.2.cloned.1.call-done, s32[16]{0:T(128)S(1)} %copy-done.3, s32[2]{0:T(128)S(1)} %iota_add_fusion), kind=kOutput, calls=%fused_computation.17 | convolution fusion | flops 12583040 | bytes 2359368 | tf_op jit(solution)/shard_map/dr,dbf->rbf/dot_general | solution.py:40
  106.9 0.1 copy.24
  106.9 28.5 %all-to-all-done = bf16[1,16,2,2,64,512]{5,4,3,2,0,1:T(8,128)(2,1)} async-done(((bf16[1,16,2,2,64,512]{5,4,3,2,0,1:T(8,128)(2,1)}), bf16[1,16,2,2,64,512]{5,4,3,2,0,1:T(8,128)(2,1)}, u32[]{:S(2)}, u32[]{:S(2)}) %all-to-all-start) | async-done | bytes 4194336 | tf_op jit(solution)/shard_map/all_to_all | solution.py:50
  135.4 33.5 %while.15 = (s32[]{:T(128)}, f32[2,2,64,512]{3,2,1,0:T(8,128)S(1)}, bf16[16,2,2,64,512]{4,3,2,1,0:T(8,128)(2,1)}, f32[16,64,512]{2,1,0:T(8,128)}, s32[]{:T(128)}, /*index=5*/s32[]{:T(128)}) while((s32[]{:T(128)}, f32[2,2,64,512]{3,2,1,0:T(8,128)S(1)}, bf16[16,2,2,64,512]{4,3,2,1,0:T(8,128)(2,1)}, f32[16,64,512]{2,1,0:T(8,128)}, ...), condition=%wide.region_2.3_spmd.clone, body=%wide.region_1.2_spmd.clone.sunk | while | flops 524291 | bytes 1704031 | solution.py:58
  135.4 0.9 dynamic-slice_bitcast_fusion.2
  136.3 1.2 fusion.38
  137.5 0.9 dynamic-slice_bitcast_fusion.2
  138.4 1.2 fusion.38
  139.6 0.9 dynamic-slice_bitcast_fusion.2
  140.5 1.2 fusion.38
  141.7 0.9 dynamic-slice_bitcast_fusion.2
  142.6 1.2 fusion.38
  143.8 0.9 dynamic-slice_bitcast_fusion.2
  144.7 1.2 fusion.38
  145.9 0.9 dynamic-slice_bitcast_fusion.2
  146.8 1.2 fusion.38
  148.0 0.9 dynamic-slice_bitcast_fusion.2
  148.9 1.2 fusion.38
  150.1 0.9 dynamic-slice_bitcast_fusion.2
  151.0 1.2 fusion.38
  152.2 0.9 dynamic-slice_bitcast_fusion.2
  153.1 1.2 fusion.38
  154.2 0.9 dynamic-slice_bitcast_fusion.2
  155.2 1.2 fusion.38
  156.3 0.9 dynamic-slice_bitcast_fusion.2
  157.3 1.2 fusion.38
  158.4 0.9 dynamic-slice_bitcast_fusion.2
  159.4 1.2 fusion.38
  160.5 0.9 dynamic-slice_bitcast_fusion.2
  161.5 1.2 fusion.38
  162.6 0.9 dynamic-slice_bitcast_fusion.2
  163.5 1.2 fusion.38
  164.7 0.9 dynamic-slice_bitcast_fusion.2
  165.6 1.2 fusion.38
  166.8 0.9 dynamic-slice_bitcast_fusion.2
  167.7 1.2 fusion.38
  168.9 0.1 divide_convert_fusion
  169.0 0.4 copy.19
  169.4 1.1 reshape.216
  170.5 10.5 %all-to-all-start.1 = ((bf16[32,2,2048]{2,1,0:T(2,128)(2,1)}), bf16[32,2,2048]{2,1,0:T(2,128)(2,1)S(1)}, u32[]{:S(2)}, u32[]{:S(2)}) async-start(bf16[32,2,2048]{2,1,0:T(2,128)(2,1)} %reshape.216), calls=%async_computation.1 | async-start | bytes 524288 | tf_op jit(solution)/shard_map/all_to_all | solution.py:68
  181.0 0.0 copy-start.1
  181.0 64.1 %fusion.1 = (bf16[16,512,512]{2,1,0:T(8,128)(2,1)}, bf16[16,512,512]{2,1,0:T(8,128)(2,1)}) fusion(f32[512]{0:T(512)S(1)} %multiply_add_fusion.2, f32[16,512]{1,0:T(8,128)S(1)} %broadcast_multiply_fusion), kind=kLoop, calls=%fused_computation.5 | loop fusion | flops 16777216 | bytes 16812032 | tf_op jit(solution)/shard_map/convert_element_type | solution.py:24
  245.2 0.4 reshape.217
  245.5 0.1 copy.20
  245.6 0.1 copy.21
  245.7 0.5 reshape.213
  246.2 2.9 %fusion.18 = bf16[16,2,4,2,512]{4,0,3,1,2:T(8,128)(2,1)S(1)} fusion(bf16[2,2,2048,16,1]{2,3,1,0,4:T(8,128)(2,1)S(1)} %reshape.213, s32[4,512]{1,0:T(4,128)S(1)} %multiply_add_fusion, s32[2048]{0:T(1024)S(1)} %multiply_add_fusion.1), kind=kOutput, calls=%fused_computation.21 | convolution fusion | flops 541196288 | bytes 540672 | tf_op jit(solution)/shard_map/kxbf,bcn->fkcxn/dot_general | solution.py:70
  249.1 0.3 copy.22
  249.4 0.2 reshape.207
  249.5 7.1 %fusion.4 = f32[16,8,512]{2,1,0:T(8,128)S(1)} fusion(bf16[16,8,1024]{2,1,0:T(8,128)(2,1)S(1)} %reshape.207, bf16[16,512,512]{2,1,0:T(8,128)(2,1)} %get-tuple-element.129, bf16[16,512,512]{2,1,0:T(8,128)(2,1)} %get-tuple-element.128), kind=kOutput, calls=%fused_computation.8 | convolution fusion | flops 167772160 | bytes 17301504 | tf_op jit(solution)/shard_map/fmq,fqp->fmp/dot_general | solution.py:74
  256.7 0.8 reshape.208
  (15 shorter events, 0.1 us)
Async XLA Ops:
  15.0 88.4 %copy-start.3 = (s32[16]{0:T(128)S(1)}, s32[16]{0:T(128)}, u32[]{:S(2)}) copy-start(s32[16]{0:T(128)} %param.11) | copy-start | bytes 196
  18.8 2.0 copy-start
  20.8 114.6 %all-to-all-start = ((bf16[1,16,2,2,64,512]{5,4,3,2,0,1:T(8,128)(2,1)}), bf16[1,16,2,2,64,512]{5,4,3,2,0,1:T(8,128)(2,1)}, u32[]{:S(2)}, u32[]{:S(2)}) async-start(bf16[1,16,2,2,64,512]{5,4,3,2,0,1:T(8,128)(2,1)} %bitcast.46), calls=%async_computation | async-start | bytes 8388608 | tf_op jit(solution)/shard_map/all_to_all | solution.py:50
  31.9 71.5 %all-gather.2.cloned.1.call-start = ((), (), s32[]{:S(2)}) async-start(), calls=%async_computation.2 | async-start | bytes 2228224 | tf_op jit(solution)/shard_map/all_gather | solution.py:36
  170.5 74.7 %all-to-all-start.1 = ((bf16[32,2,2048]{2,1,0:T(2,128)(2,1)}), bf16[32,2,2048]{2,1,0:T(2,128)(2,1)S(1)}, u32[]{:S(2)}, u32[]{:S(2)}) async-start(bf16[32,2,2048]{2,1,0:T(2,128)(2,1)} %reshape.216), calls=%async_computation.1 | async-start | bytes 524288 | tf_op jit(solution)/shard_map/all_to_all | solution.py:68
  181.0 64.1 %copy-start.1 = (s32[2048]{0:T(1024)S(1)}, s32[2048]{0:T(1024)}, u32[]{:S(2)}) copy-start(s32[2048]{0:T(1024)} %param.13) | copy-start | bytes 24580
  181.0 64.1 %copy-start.2 = (s32[2048]{0:T(1024)S(1)}, s32[2048]{0:T(1024)}, u32[]{:S(2)}) copy-start(s32[2048]{0:T(1024)} %param.12) | copy-start | bytes 24580
Sparse Core Ops, SparseCore 0:
  34.9 68.4 all-gather.1
where the time goes:
time: 266 us; the launch traced here: 264 us
  waiting for transfers between devices  99.8 us (38%)
  other arithmetic  88.1 us (33%)
  local copies, waits for them, and re-layouts  25.4 us (10%)
  starting transfers between devices  21.7 us (8%)
  between operations  15.6 us (6%)
  matrix products  13.5 us (5%)
    all_gather x1, waiting for transfers between devices, local(): all_weights = lax.all_gather(day_weight, 'day', axis=0, tiled=True)  70.6 us
    convert_element_type x1, other arithmetic, ns_table(): jnp.cos(phase).astype(jnp.bfloat16)  64.1 us
    all_to_all x1, waiting for transfers between devices, local(): lax.all_to_all(outgoing, 'day', split_axis=1, concat_axis=0, tiled=True)  28.5 us
    add x16, other arithmetic, add_day(): return running + one_day.astype(jnp.float32) * weight_now[None, None]  18.5 us
    mul x16, local copies, waits for them, and re-layouts, add_day(): return running + one_day.astype(jnp.float32) * weight_now[None, None]  14.7 us
    all_to_all x1, starting transfers between devices, local(): lax.all_to_all(outgoing, 'day', split_axis=1, concat_axis=0, tiled=True)  11.2 us
    all_to_all x1, starting transfers between devices, local(): block = lax.all_to_all(stack, 'bl', split_axis=3, concat_axis=2, tiled=True)  10.5 us
    dot_general x1, matrix products, local(): jnp.einsum('fmq,fqp->fmp', grid, table, preferred_element_type=jnp.float32)  7.15 us
  transfers between devices with their start and end apart: 3, of which 2 were waited for; matrix products, arithmetic and copies ran while one was open for 26% of the time, Pallas kernels for 0%

commit v1 on v0

v1 whole, which is shorter than its diff:
```python
import jax
import jax.numpy as jnp
from jax import lax
from jax.experimental import pallas as pl
from jax.experimental.pallas import tpu as pltpu
from jax.sharding import PartitionSpec as P

FREQ = 512
PAIRS = 4
NSEP = 512
PIXELS = 512
HALF = PIXELS // 2
RA = 32
RA_DEV = 2
SAMPLES = 16
DAYS = 16
BASES = 2048
N_BL = 32
BASE_LOC = BASES // N_BL
BAND = FREQ // N_BL
COARSE = 32
FINE = NSEP // COARSE
CHIPS = 8
HELD = 8
SCALE = 128.0

F32 = jnp.float32
BF16 = jnp.bfloat16
F16 = jnp.float16
MIB = 1 << 20

phase_scale = 2.0 * 3.141592653589793 * 0.3048 / 299.792458


def bins_below(offset, core):
    return 2 * (offset >> 2) + jnp.clip((offset & 3) - 2 * core, 0, 2)


def select_kernel(offset_ref, vis_ref, out_ref, sems):
    day = lax.axis_index("day")
    other = 1 - (day & 1)
    offset = offset_ref[day]
    first = bins_below(offset, other)
    copies = []
    for k in range(HELD):
        owned = first + k
        sample = 4 * (owned >> 1) + 2 * other + (owned & 1) - offset
        copies.append(
            pltpu.make_async_copy(
                vis_ref.at[sample], out_ref.at[owned & (HELD - 1)], sems.at[k]
            )
        )
        copies[-1].start()
    for copy in copies:
        copy.wait()


def select(day_offset, visibility):
    return pl.pallas_call(
        select_kernel,
        in_specs=[pl.BlockSpec(memory_space=pltpu.SMEM), pl.BlockSpec(memory_space=pl.ANY)],
        out_specs=pl.BlockSpec(memory_space=pltpu.VMEM),
        out_shape=jax.ShapeDtypeStruct((HELD, 2, BASE_LOC, FREQ), BF16),
        scratch_shapes=[pltpu.SemaphoreType.DMA((HELD,))],
        compiler_params=pltpu.CompilerParams(vmem_limit_bytes=8 * MIB),
        name="select",
    )(day_offset, visibility[0])


def chip_kernel(offset_ref, vis_ref, weight_ref, other_vis_ref, other_weight_ref, out_ref):
    day = lax.axis_index("day")
    core = day & 1
    chip = day >> 1
    offset = offset_ref[day]
    first = bins_below(offset_ref[day ^ 1], core)
    weight = weight_ref[...] * SCALE
    other_weight = other_weight_ref[...] * SCALE

    def one_bin(at, _):
        owned = 2 * ((chip + (at >> 1)) & (CHIPS - 1)) + (at & 1)
        sample = 4 * (owned >> 1) + 2 * core + (owned & 1) - offset
        valid = jnp.logical_and(sample >= 0, sample < SAMPLES)
        held = jnp.logical_and(owned >= first, owned < first + HELD)
        sample = jnp.clip(sample, 0, SAMPLES - 1)
        own = weight * jnp.where(valid, 1.0, 0.0)
        other = other_weight * jnp.where(held, 1.0, 0.0)
        for x in range(2):
            out_ref[at, x] = (
                vis_ref[sample, x].astype(F32) * own
                + other_vis_ref[owned & (HELD - 1), x].astype(F32) * other
            )
        return 0

    lax.fori_loop(0, 2 * CHIPS, one_bin, 0)


def chip_sums(day_offset, visibility, day_weight, other_vis, other_weight):
    rows = 16
    weight_spec = pl.BlockSpec((rows, FREQ), lambda i: (i, 0))
    return pl.pallas_call(
        chip_kernel,
        grid=(BASE_LOC // rows,),
        in_specs=[
            pl.BlockSpec(memory_space=pltpu.SMEM),
            pl.BlockSpec((SAMPLES, 2, rows, FREQ), lambda i: (0, 0, i, 0)),
            weight_spec,
            pl.BlockSpec((HELD, 2, rows, FREQ), lambda i: (0, 0, i, 0)),
            weight_spec,
        ],
        out_specs=pl.BlockSpec((2 * CHIPS, 2, rows, FREQ), lambda i: (0, 0, i, 0)),
        out_shape=jax.ShapeDtypeStruct((2 * CHIPS, 2, BASE_LOC, FREQ), F32),
        compiler_params=pltpu.CompilerParams(vmem_limit_bytes=16 * MIB),
        name="chip_sums",
    )(day_offset, visibility[0], day_weight[0], other_vis, other_weight)


def reduce_ring(chip_sum):
    up = [(2 * y + c, 2 * ((y + 1) % CHIPS) + c) for y in range(CHIPS) for c in range(2)]
    down = [(b, a) for a, b in up]
    streams = [[up, 0, 4, 1], [down, 1, 4, -1], [up, 1, 3, 1], [down, 0, 3, -1]]
    arrived = [None] * 4
    for step in range(4):
        for at, (pairs, which, hops, way) in enumerate(streams):
            if step >= hops:
                continue
            distance = (way * (hops - step)) % CHIPS
            own = chip_sum[2 * distance + which]
            if step:
                own = own + arrived[at].astype(F32)
            arrived[at] = lax.ppermute(own.astype(F16), "day", pairs)
    low = chip_sum[0] + arrived[0].astype(F32) + arrived[3].astype(F32)
    high = chip_sum[1] + arrived[1].astype(F32) + arrived[2].astype(F32)
    return low, high


def table_kernel(cos_a_ref, sin_a_ref, cos_b_ref, sin_b_ref, out_ref):
    cos_b = cos_b_ref[0]
    sin_b = sin_b_ref[0]
    for a in range(COARSE):
        cos_a = cos_a_ref[0, a : a + 1, :]
        sin_a = sin_a_ref[0, a : a + 1, :]
        rows = pl.ds(a * FINE, FINE)
        out_ref[0, rows, :HALF] = (cos_a * cos_b - sin_a * sin_b).astype(BF16)
        out_ref[0, rows, HALF:] = (-(sin_a * cos_b + cos_a * sin_b)).astype(BF16)


def ns_table():
    freq_at = (lax.axis_index("bl") * BAND + jnp.arange(BAND)).astype(F32)
    factor = phase_scale * (800.0 - 400.0 * (freq_at + 0.5) / FREQ)
    sine_dir = -1.0 + 2.0 * (jnp.arange(HALF).astype(F32) + 0.5) / PIXELS
    coarse = (jnp.arange(COARSE) * FINE - NSEP // 2).astype(F32)
    fine = jnp.arange(FINE).astype(F32)
    phase_a = factor[:, None, None] * coarse[None, :, None] * sine_dir[None, None, :]
    phase_b = factor[:, None, None] * fine[None, :, None] * sine_dir[None, None, :]
    spec_a = pl.BlockSpec((1, COARSE, HALF), lambda f: (f, 0, 0))
    spec_b = pl.BlockSpec((1, FINE, HALF), lambda f: (f, 0, 0))
    return pl.pallas_call(
        table_kernel,
        grid=(BAND,),
        in_specs=[spec_a, spec_a, spec_b, spec_b],
        out_specs=pl.BlockSpec((1, NSEP, 2 * HALF), lambda f: (f, 0, 0)),
        out_shape=jax.ShapeDtypeStruct((BAND, NSEP, 2 * HALF), BF16),
        compiler_params=pltpu.CompilerParams(vmem_limit_bytes=16 * MIB),
        cost_estimate=pl.CostEstimate(
            flops=6 * BAND * NSEP * HALF, bytes_accessed=4 * BAND * NSEP * HALF, transcendentals=0
        ),
        name="table",
    )(jnp.cos(phase_a), jnp.sin(phase_a), jnp.cos(phase_b), jnp.sin(phase_b))


def inverse_total(day_offset, all_weights):
    bins = lax.axis_index("day") * RA_DEV + jnp.arange(RA_DEV)
    sample = bins[:, None] - day_offset[None, :]
    valid = jnp.logical_and(sample >= 0, sample < SAMPLES).astype(F32)
    total = jnp.sum(valid[:, :, None, None] * all_weights[None].astype(F32), axis=1)
    return (1.0 / SCALE) / total


def pack_blocks(pieces, out_ref, rows):
    lane_group = lax.broadcasted_iota(jnp.int32, (8, 128), 1) // BAND
    for tile in range(FREQ // 128):
        parts = [piece[:, tile * 128 : (tile + 1) * 128] for piece in pieces]
        for step in (4, 2, 1):
            keep = (lane_group & step) == 0
            mixed = list(parts)
            for low in range(8):
                if low & step:
                    continue
                high = low | step
                mixed[low] = jnp.where(keep, parts[low], pltpu.roll(parts[high], step * BAND, 1))
                mixed[high] = jnp.where(
                    keep, pltpu.roll(parts[low], 128 - step * BAND, 1), parts[high]
                )
            parts = mixed
        for group in range(8):
            out_ref[tile * 8 + group, rows, :] = parts[group].astype(BF16)


def pack_kernel(low_ref, high_ref, inverse_ref, out_ref):
    half = BASE_LOC // 2
    for first in range(0, half, 16):
        for sub in range(0, 16, 8):
            rows = pl.ds(first + sub, 8)
            pieces = []
            for x in range(2):
                for r in range(RA_DEV):
                    for hi in range(2):
                        rows_in = pl.ds(hi * half + first + sub, 8)
                        pieces.append(
                            (low_ref, high_ref)[r][x, rows_in, :] * inverse_ref[r, rows_in, :]
                        )
            pack_blocks(pieces, out_ref, rows)


def pack(low, high, inverse):
    vmem = pl.BlockSpec(memory_space=pltpu.VMEM)
    return pl.pallas_call(
        pack_kernel,
        in_specs=[vmem, vmem, vmem],
        out_specs=vmem,
        out_shape=jax.ShapeDtypeStruct((N_BL, BASE_LOC // 2, 128), BF16),
        compiler_params=pltpu.CompilerParams(vmem_limit_bytes=16 * MIB),
        name="pack",
    )(low, high, inverse)


def beam_kernel(block_ref, pair_ref, sep_ref, table_ref, out_ref, grid_ref):
    flat = BASES // 2
    rows = RA_DEV * PAIRS

    @pl.when(pl.program_id(0) == 0)
    def _():
        turned = block_ref[...].astype(F32).reshape(flat, 128).T
        total = jnp.zeros((2 * rows * BAND, NSEP), F32)
        for hi in range(2):
            picked = [
                turned[(group * 2 + hi) * BAND : (group * 2 + hi + 1) * BAND] for group in range(4)
            ]
            pair = pair_ref[hi : hi + 1, :]
            masked = jnp.concatenate(
                [jnp.where(pair == c, part, 0.0) for part in picked for c in range(PAIRS)], axis=0
            ).astype(BF16)
            sep = sep_ref[:, hi : hi + 1]
            onehot = jnp.where(
                sep == lax.broadcasted_iota(jnp.int32, (flat, NSEP), 1), 1.0, 0.0
            ).astype(BF16)
            total = total + jnp.dot(masked, onehot, preferred_element_type=F32)
        for tile in range(NSEP // 128):
            grid_ref[tile] = total[:, tile * 128 : (tile + 1) * 128]

    flip = (
        lax.broadcasted_iota(jnp.int32, (HALF, HALF), 0)
        + lax.broadcasted_iota(jnp.int32, (HALF, HALF), 1)
        == HALF - 1
    )
    flip = jnp.where(flip, 1.0, 0.0).astype(BF16)
    count = table_ref.shape[0]
    odd_part = []
    for f in range(count):
        f_at = pl.program_id(0) * count + f
        cells = jnp.concatenate(
            [
                grid_ref[tile, pl.ds(f_at, 2 * rows, stride=BAND), :]
                for tile in range(NSEP // 128)
            ],
            axis=1,
        ).astype(BF16)
        even = jnp.dot(cells, table_ref[f], preferred_element_type=F32)
        cos_part = even[:rows, :HALF]
        sin_part = even[rows:, HALF:]
        out_ref[f, :, :HALF] = cos_part + sin_part
        odd_part.append(cos_part - sin_part)
    rest = jnp.concatenate(odd_part, axis=0)
    turned = jnp.zeros(rest.shape, F32)
    for _ in range(3):
        piece = rest.astype(BF16)
        rest = rest - piece.astype(F32)
        turned = turned + jnp.dot(piece, flip, preferred_element_type=F32)
    for f in range(count):
        out_ref[f, :, HALF:] = turned[f * rows : (f + 1) * rows]


def beam(block, pair_index, sep_index, table):
    flat = BASES // 2
    count = 4
    pair = pair_index.reshape(N_BL, 2, BASE_LOC // 2).transpose(1, 0, 2).reshape(2, flat)
    sep = sep_index.reshape(N_BL, 2, BASE_LOC // 2).transpose(0, 2, 1).reshape(flat, 2)
    whole = lambda shape: pl.BlockSpec(shape, lambda i: (0,) * len(shape))
    return pl.pallas_call(
        beam_kernel,
        grid=(BAND // count,),
        in_specs=[
            whole((N_BL, BASE_LOC // 2, 128)),
            whole((2, flat)),
            whole((flat, 2)),
            pl.BlockSpec((count, NSEP, 2 * HALF), lambda i: (i, 0, 0)),
        ],
        out_specs=pl.BlockSpec((count, RA_DEV * PAIRS, PIXELS), lambda i: (i, 0, 0)),
        out_shape=jax.ShapeDtypeStruct((BAND, RA_DEV * PAIRS, PIXELS), F32),
        scratch_shapes=[pltpu.VMEM((NSEP // 128, 2 * RA_DEV * PAIRS * BAND, 128), F32)],
        compiler_params=pltpu.CompilerParams(vmem_limit_bytes=32 * MIB),
        name="beam",
    )(block, pair, sep, table)


def day_stage(visibility, day_weight, day_offset):
    swap = [(d, d ^ 1) for d in range(DAYS)]
    other_vis = lax.ppermute(select(day_offset, visibility), "day", swap)
    other_weight = lax.ppermute(day_weight[0], "day", swap)
    all_weights = lax.all_gather(day_weight.astype(F16), "day", axis=0, tiled=True)
    low, high = reduce_ring(
        chip_sums(day_offset, visibility, day_weight, other_vis, other_weight)
    )
    return low, high, inverse_total(day_offset, all_weights)


def beam_stage(low, high, inverse, pair_index, sep_index):
    table = ns_table()
    packed = pack(low, high, inverse)
    block = lax.all_to_all(packed, "bl", split_axis=0, concat_axis=0, tiled=True)
    return beam(block, pair_index, sep_index, table)


def local(visibility, day_weight, day_offset, pair_index, sep_index):
    low, high, inverse = day_stage(visibility, day_weight, day_offset)
    result = beam_stage(low, high, inverse, pair_index, sep_index)
    return result.reshape(BAND, RA_DEV, PAIRS, PIXELS)


def solution(mesh):
    return jax.shard_map(
        local,
        mesh=mesh,
        in_specs=(P("day", None, None, "bl", None), P("day", "bl", None), P(), P(), P()),
        out_specs=P("bl", "day", None, None),
        check_vma=False,
    )
```

time: 266 us -> 149 us (0.56)
  the two profiles are of different devices: /device:TPU:1 before, /device:TPU:56 now
where the time goes in v1:
time: 149 us; the launch traced here: 148 us
  starting transfers between devices  61.1 us (41%)
  waiting for transfers between devices  30.6 us (21%)
  blocking collectives  19 us (13%)
  local copies, waits for them, and re-layouts  13.1 us (9%)
  other arithmetic  11.9 us (8%)
  Pallas kernels  11.8 us (8%)
    ppermute x14, starting transfers between devices, reduce_ring(): arrived[at] = lax.ppermute(own.astype(F16), 'day', pairs)  46.1 us
    ppermute x14, waiting for transfers between devices, reduce_ring(): arrived[at] = lax.ppermute(own.astype(F16), 'day', pairs)  27 us
    all_gather x1, blocking collectives, day_stage(): lax.all_gather(day_weight.astype(F16), 'day', axis=0, tiled=True)  19 us
    all_to_all x1, starting transfers between devices, beam_stage(): lax.all_to_all(packed, 'bl', split_axis=0, concat_axis=0, tiled=True)  10.7 us
    unnamed x24, local copies, waits for them, and re-layouts  10.5 us
    convert_element_type x6, other arithmetic, reduce_ring(): arrived[at] = lax.ppermute(own.astype(F16), 'day', pairs)  5.28 us
    pallas_call x1, Pallas kernels, beam(): pl.pallas_call(beam_kernel, grid=(BAND // count,), in_specs=[whole((N_BL,...  3.29 us
  transfers between devices with their start and end apart: 17, of which 10 were waited for; matrix products, arithmetic and copies ran while one was open for 5% of the time, Pallas kernels for 2%

profile of v1, /device:TPU:56, one launch (start us, length us, event | category | flops | bytes accessed | tf_op | source)
XLA Modules:
  0.0 147.9 jit_solution(2257450247347102144)
XLA Ops:
  0.0 1.6 %copy-done.3 = bf16[1,16,2,64,512]{4,3,2,1,0:T(8,128)(2,1)S(1)} copy-done((bf16[1,16,2,64,512]{4,3,2,1,0:T(8,128)(2,1)S(1)}, bf16[1,16,2,64,512]{4,3,2,1,0:T(8,128)(2,1)}, u32[]{:S(2)}) %copy-start.3) | copy-done | bytes 2097176
  1.6 0.7 copy-done.7
  2.2 2.0 %select.1 = bf16[8,2,64,512]{3,2,1,0:T(8,128)(2,1)S(1)} custom-call(s32[16]{0:T(128)S(1)} %copy-done.7, bf16[16,2,64,512]{3,2,1,0:T(8,128)(2,1)S(1)} %bitcast.85), custom_call_target="tpu_custom_call" | custom-call | tf_op jit(solution)/shard_map/select/pallas_call | solution.py:59
  4.3 1.9 %collective-permute-start = (bf16[8,2,64,512]{3,2,1,0:T(8,128)(2,1)S(1)}, bf16[8,2,64,512]{3,2,1,0:T(8,128)(2,1)S(1)}, u32[]{:S(2)}, u32[]{:S(2)}) collective-permute-start(bf16[8,2,64,512]{3,2,1,0:T(8,128)(2,1)S(1)} %select.1), channel_id=1, source_target_pairs={{0,32},{32,0},{64,96},{96,64},{128,160},{160,128},{192,224},{224,1... | collective-permute-start | bytes 3145736 | tf_op jit(solution)/shard_map/ppermute | solution.py:308
  6.2 2.4 %collective-permute-start.1 = (f32[64,512]{1,0:T(8,128)}, f32[64,512]{1,0:T(8,128)S(1)}, u32[]{:S(2)}, u32[]{:S(2)}) collective-permute-start(f32[64,512]{1,0:T(8,128)} %bitcast.88), channel_id=1, source_target_pairs={{0,32},{32,0},{64,96},{96,64},{128,160},{160,128},{192,224},{224,1... | collective-permute-start | bytes 393224 | tf_op jit(solution)/shard_map/ppermute | solution.py:309
  8.6 1.2 collective-permute-done.1.other_weight_ref
  9.8 0.9 copy-done.5
  10.7 0.7 copy-done.8
  11.4 2.7 %chip_sums.1 = f32[16,2,64,512]{3,2,1,0:T(8,128)S(1)} custom-call(s32[16]{0:T(128)S(1)} %copy-done.8, bf16[16,2,64,512]{3,2,1,0:T(8,128)(2,1)S(1)} %bitcast.86, f32[64,512]{1,0:T(8,128)S(1)} %bitcast.89, bf16[8,2,64,512]{3,2,1,0:T(8,128)(2,1)S(1)} %collective-permute-done.other_vis_ref, f32[64,512]{1,0:T(8,128)S(1)} %collective-permute-done.1.other_weight_ref), custom_call_target="tpu_custom_call" | custom-call | tf_op jit(solution)/shard_map/chip_sums/pallas_call | solution.py:100
  14.1 0.0 copy-start.6
  14.1 0.6 convert.6
  14.7 0.0 copy-start.9
  14.7 1.2 slice_bitcast_fusion.13
  15.9 3.3 %collective-permute-start.9 = (f16[2,64,512]{2,1,0:T(8,128)(2,1)S(1)}, f16[2,64,512]{2,1,0:T(8,128)(2,1)S(1)}, u32[]{:S(2)}, u32[]{:S(2)}) collective-permute-start(f16[2,64,512]{2,1,0:T(8,128)(2,1)S(1)} %get-tuple-element.12), channel_id=1, source_target_pairs={{64,0},{96,32},{128,64},{160,96},{192,128},{224,160},{256,192},{28... | collective-permute-start | bytes 393224 | tf_op jit(solution)/shard_map/ppermute | solution.py:130
  19.2 7.8 %collective-permute-done.9 = f16[2,64,512]{2,1,0:T(8,128)(2,1)S(1)} collective-permute-done((f16[2,64,512]{2,1,0:T(8,128)(2,1)S(1)}, f16[2,64,512]{2,1,0:T(8,128)(2,1)S(1)}, u32[]{:S(2)}, u32[]{:S(2)}) %collective-permute-start.9) | collective-permute-done | bytes 131104 | tf_op jit(solution)/shard_map/ppermute | solution.py:130
  27.0 1.9 %collective-permute-start.10 = (f16[2,64,512]{2,1,0:T(8,128)(2,1)S(1)}, f16[2,64,512]{2,1,0:T(8,128)(2,1)S(1)}, u32[]{:S(2)}, u32[]{:S(2)}) collective-permute-start(f16[2,64,512]{2,1,0:T(8,128)(2,1)S(1)} %fusion.5), channel_id=1, source_target_pairs={{64,0},{96,32},{128,64},{160,96},{192,128},{224,160},{256,192},{28... | collective-permute-start | bytes 393224 | tf_op jit(solution)/shard_map/ppermute | solution.py:130
  29.0 19.0 %all-gather.1 = f16[16,64,512]{2,1,0:T(8,128)(2,1)S(1)} all-gather(f16[1,64,512]{2,1,0:T(8,128)(2,1)S(1)} %convert_element_type.161), channel_id=1, replica_groups=mesh['day'=16,'bl'=32] {'day'}, dimensions={0}, use_global_device_ids=true | all-gather | bytes 1114112 | tf_op jit(solution)/shard_map/all_gather | solution.py:310
  48.0 0.3 convert_element_type.162
  48.3 4.9 %collective-permute-start.13 = (f16[2,64,512]{2,1,0:T(8,128)(2,1)}, f16[2,64,512]{2,1,0:T(8,128)(2,1)S(1)}, u32[]{:S(2)}, u32[]{:S(2)}) collective-permute-start(f16[2,64,512]{2,1,0:T(8,128)(2,1)} %get-tuple-element.13), channel_id=1, source_target_pairs={{0,64},{32,96},{64,128},{96,160},{128,192},{160,224},{192,256},{22... | collective-permute-start | bytes 393224 | tf_op jit(solution)/shard_map/ppermute | solution.py:130
  53.1 1.0 fusion.7
  54.1 1.9 %collective-permute-start.11 = (f16[2,64,512]{2,1,0:T(8,128)(2,1)S(1)}, f16[2,64,512]{2,1,0:T(8,128)(2,1)S(1)}, u32[]{:S(2)}, u32[]{:S(2)}) collective-permute-start(f16[2,64,512]{2,1,0:T(8,128)(2,1)S(1)} %fusion.7), channel_id=1, source_target_pairs={{64,0},{96,32},{128,64},{160,96},{192,128},{224,160},{256,192},{28... | collective-permute-start | bytes 393224 | tf_op jit(solution)/shard_map/ppermute | solution.py:130
  56.1 0.1 and_convert_fusion
  56.1 0.5 collective-permute-done.13
  56.7 6.0 %collective-permute-done.11 = f16[2,64,512]{2,1,0:T(8,128)(2,1)S(1)} collective-permute-done((f16[2,64,512]{2,1,0:T(8,128)(2,1)S(1)}, f16[2,64,512]{2,1,0:T(8,128)(2,1)S(1)}, u32[]{:S(2)}, u32[]{:S(2)}) %collective-permute-start.11) | collective-permute-done | bytes 131104 | tf_op jit(solution)/shard_map/ppermute | solution.py:130
  62.7 1.1 fusion.9
  63.8 0.0 copy-start.10
  63.8 1.9 %collective-permute-start.14 = (f16[2,64,512]{2,1,0:T(8,128)(2,1)S(1)}, f16[2,64,512]{2,1,0:T(8,128)(2,1)S(1)}, u32[]{:S(2)}, u32[]{:S(2)}) collective-permute-start(f16[2,64,512]{2,1,0:T(8,128)(2,1)S(1)} %get-tuple-element.9), channel_id=1, source_target_pairs={{0,64},{32,96},{64,128},{96,160},{128,192},{160,224},{192,256},{22... | collective-permute-start | bytes 393224 | tf_op jit(solution)/shard_map/ppermute | solution.py:130
  65.8 0.3 multiply_reduce_fusion
  66.1 0.0 copy-start.11
  66.1 1.9 %collective-permute-start.2 = (f16[2,64,512]{2,1,0:T(8,128)(2,1)}, f16[2,64,512]{2,1,0:T(8,128)(2,1)S(1)}, u32[]{:S(2)}, u32[]{:S(2)}) collective-permute-start(f16[2,64,512]{2,1,0:T(8,128)(2,1)} %get-tuple-element.15), channel_id=1, source_target_pairs={{0,64},{32,96},{64,128},{96,160},{128,192},{160,224},{192,256},{22... | collective-permute-start | bytes 393224 | tf_op jit(solution)/shard_map/ppermute | solution.py:130
  68.1 3.9 %collective-permute-start.6 = (f16[2,64,512]{2,1,0:T(8,128)(2,1)S(1)}, f16[2,64,512]{2,1,0:T(8,128)(2,1)S(1)}, u32[]{:S(2)}, u32[]{:S(2)}) collective-permute-start(f16[2,64,512]{2,1,0:T(8,128)(2,1)S(1)} %get-tuple-element.14), channel_id=1, source_target_pairs={{64,0},{96,32},{128,64},{160,96},{192,128},{224,160},{256,192},{28... | collective-permute-start | bytes 393224 | tf_op jit(solution)/shard_map/ppermute | solution.py:130
  72.0 3.9 %collective-permute-start.12 = (f16[2,64,512]{2,1,0:T(8,128)(2,1)S(1)}, f16[2,64,512]{2,1,0:T(8,128)(2,1)S(1)}, u32[]{:S(2)}, u32[]{:S(2)}) collective-permute-start(f16[2,64,512]{2,1,0:T(8,128)(2,1)S(1)} %get-tuple-element.8), channel_id=1, source_target_pairs={{64,0},{96,32},{128,64},{160,96},{192,128},{224,160},{256,192},{28... | collective-permute-start | bytes 393224 | tf_op jit(solution)/shard_map/ppermute | solution.py:130
  75.9 1.0 fusion.3
  76.9 3.1 %collective-permute-start.15 = (f16[2,64,512]{2,1,0:T(8,128)(2,1)S(1)}, f16[2,64,512]{2,1,0:T(8,128)(2,1)S(1)}, u32[]{:S(2)}, u32[]{:S(2)}) collective-permute-start(f16[2,64,512]{2,1,0:T(8,128)(2,1)S(1)} %fusion.3), channel_id=1, source_target_pairs={{0,64},{32,96},{64,128},{96,160},{128,192},{160,224},{192,256},{22... | collective-permute-start | bytes 393224 | tf_op jit(solution)/shard_map/ppermute | solution.py:130
  80.2 3.6 %collective-permute-done.15 = f16[2,64,512]{2,1,0:T(8,128)(2,1)S(1)} collective-permute-done((f16[2,64,512]{2,1,0:T(8,128)(2,1)S(1)}, f16[2,64,512]{2,1,0:T(8,128)(2,1)S(1)}, u32[]{:S(2)}, u32[]{:S(2)}) %collective-permute-start.15) | collective-permute-done | bytes 131104 | tf_op jit(solution)/shard_map/ppermute | solution.py:130
  83.8 1.2 fusion.11
  85.0 4.3 %collective-permute-start.3 = (f16[2,64,512]{2,1,0:T(8,128)(2,1)S(1)}, f16[2,64,512]{2,1,0:T(8,128)(2,1)S(1)}, u32[]{:S(2)}, u32[]{:S(2)}) collective-permute-start(f16[2,64,512]{2,1,0:T(8,128)(2,1)S(1)} %get-tuple-element.7), channel_id=1, source_target_pairs={{0,64},{32,96},{64,128},{96,160},{128,192},{160,224},{192,256},{22... | collective-permute-start | bytes 393224 | tf_op jit(solution)/shard_map/ppermute | solution.py:130
  89.4 1.9 %collective-permute-start.7 = (f16[2,64,512]{2,1,0:T(8,128)(2,1)S(1)}, f16[2,64,512]{2,1,0:T(8,128)(2,1)S(1)}, u32[]{:S(2)}, u32[]{:S(2)}) collective-permute-start(f16[2,64,512]{2,1,0:T(8,128)(2,1)S(1)} %get-tuple-element.6), channel_id=1, source_target_pairs={{64,0},{96,32},{128,64},{160,96},{192,128},{224,160},{256,192},{28... | collective-permute-start | bytes 393224 | tf_op jit(solution)/shard_map/ppermute | solution.py:130
  91.3 0.6 collective-permute-done.3
  91.9 1.0 fusion.19
  92.9 5.6 %collective-permute-start.4 = (f16[2,64,512]{2,1,0:T(8,128)(2,1)S(1)}, f16[2,64,512]{2,1,0:T(8,128)(2,1)S(1)}, u32[]{:S(2)}, u32[]{:S(2)}) collective-permute-start(f16[2,64,512]{2,1,0:T(8,128)(2,1)S(1)} %fusion.19), channel_id=1, source_target_pairs={{0,64},{32,96},{64,128},{96,160},{128,192},{160,224},{192,256},{22... | collective-permute-start | bytes 393224 | tf_op jit(solution)/shard_map/ppermute | solution.py:130
  98.5 0.1 broadcast_multiply_fusion.1
  98.5 2.4 %collective-permute-done.4 = f16[2,64,512]{2,1,0:T(8,128)(2,1)S(1)} collective-permute-done((f16[2,64,512]{2,1,0:T(8,128)(2,1)S(1)}, f16[2,64,512]{2,1,0:T(8,128)(2,1)S(1)}, u32[]{:S(2)}, u32[]{:S(2)}) %collective-permute-start.4) | collective-permute-done | bytes 131104 | tf_op jit(solution)/shard_map/ppermute | solution.py:130
  101.0 1.1 fusion.21
  102.1 5.6 %collective-permute-start.5 = (f16[2,64,512]{2,1,0:T(8,128)(2,1)S(1)}, f16[2,64,512]{2,1,0:T(8,128)(2,1)S(1)}, u32[]{:S(2)}, u32[]{:S(2)}) collective-permute-start(f16[2,64,512]{2,1,0:T(8,128)(2,1)S(1)} %get-tuple-element.10), channel_id=1, source_target_pairs={{0,64},{32,96},{64,128},{96,160},{128,192},{160,224},{192,256},{22... | collective-permute-start | bytes 393224 | tf_op jit(solution)/shard_map/ppermute | solution.py:130
  107.7 1.9 %collective-permute-start.8 = (f16[2,64,512]{2,1,0:T(8,128)(2,1)S(1)}, f16[2,64,512]{2,1,0:T(8,128)(2,1)S(1)}, u32[]{:S(2)}, u32[]{:S(2)}) collective-permute-start(f16[2,64,512]{2,1,0:T(8,128)(2,1)S(1)} %get-tuple-element.11), channel_id=1, source_target_pairs={{64,0},{96,32},{128,64},{160,96},{192,128},{224,160},{256,192},{28... | collective-permute-start | bytes 393224 | tf_op jit(solution)/shard_map/ppermute | solution.py:130
  109.6 0.1 broadcast_multiply_fusion
  109.7 0.5 collective-permute-done.5
  110.2 5.6 %collective-permute-done.8 = f16[2,64,512]{2,1,0:T(8,128)(2,1)S(1)} collective-permute-done((f16[2,64,512]{2,1,0:T(8,128)(2,1)S(1)}, f16[2,64,512]{2,1,0:T(8,128)(2,1)S(1)}, u32[]{:S(2)}, u32[]{:S(2)}) %collective-permute-start.8) | collective-permute-done | bytes 131104 | tf_op jit(solution)/shard_map/ppermute | solution.py:130
  115.7 1.0 fusion.23.low_ref
  116.7 1.4 pack.1
  118.2 10.7 %all-to-all-start = ((bf16[32,32,128]{2,1,0:T(8,128)(2,1)}), bf16[32,32,128]{2,1,0:T(8,128)(2,1)S(1)}, u32[]{:S(2)}, u32[]{:S(2)}) async-start(bf16[32,32,128]{2,1,0:T(8,128)(2,1)} %pack.1), calls=%async_computation | async-start | bytes 524288 | tf_op jit(solution)/shard_map/all_to_all | solution.py:320
  128.9 0.1 reshape.147
  129.0 0.3 copy.11
  129.3 0.1 reshape.145
  129.4 0.1 reshape.146.pair_ref
  129.5 1.0 multiply_sine_fusion.1
  130.5 1.9 %multiply_sine_fusion = (f32[16,32,256]{2,1,0:T(8,128)S(1)}, f32[16,32,256]{2,1,0:T(8,128)S(1)}) fusion(f32[256]{0:T(256)S(1)} %multiply_add_fusion, f32[16,32]{1,0:T(8,128)S(1)} %broadcast_multiply_fusion.1), kind=kLoop, calls=%fused_computation.1 | loop fusion | flops 131072 | bytes 1051648 | tf_op jit(solution)/shard_map/sin | solution.py:168
  132.4 2.4 %table.1.table_ref = bf16[16,512,512]{2,1,0:T(8,128)(2,1)S(1)} custom-call(f32[16,32,256]{2,1,0:T(8,128)S(1)} %get-tuple-element.19.cos_a_ref, f32[16,32,256]{2,1,0:T(8,128)S(1)} %get-tuple-element.18.sin_a_ref, f32[16,16,256]{2,1,0:T(8,128)S(1)} %get-tuple-element.17.cos_b_ref, f32[16,16,256]{2,1,0:T(8,128)S(1)} %get-tuple-element.16.sin_b_ref), custom_call_target="tpu_custom_call" | custom-call | flops 12582912 | bytes 8388608 | tf_op jit(solution)/shard_map/table/pallas_call | solution.py:157
  134.8 3.3 %copy-done = bf16[16,512,512]{2,1,0:T(8,128)(2,1)} copy-done((bf16[16,512,512]{2,1,0:T(8,128)(2,1)}, bf16[16,512,512]{2,1,0:T(8,128)(2,1)S(1)}, u32[]{:S(2)}) %copy-start) | copy-done | bytes 8388632
  138.1 2.4 %all-to-all-done.block_ref = bf16[32,32,128]{2,1,0:T(8,128)(2,1)S(1)} async-done(((bf16[32,32,128]{2,1,0:T(8,128)(2,1)}), bf16[32,32,128]{2,1,0:T(8,128)(2,1)S(1)}, u32[]{:S(2)}, u32[]{:S(2)}) %all-to-all-start) | async-done | bytes 262176 | tf_op jit(solution)/shard_map/all_to_all | solution.py:320
  140.5 3.4 %copy-done.1 = bf16[16,512,512]{2,1,0:T(8,128)(2,1)S(1)} copy-done((bf16[16,512,512]{2,1,0:T(8,128)(2,1)S(1)}, bf16[16,512,512]{2,1,0:T(8,128)(2,1)}, u32[]{:S(2)}) %copy-start.1) | copy-done | bytes 8388632
  143.8 3.3 %beam.1 = f32[16,8,512]{2,1,0:T(8,128)S(1)} custom-call(bf16[32,32,128]{2,1,0:T(8,128)(2,1)S(1)} %all-to-all-done.block_ref, s32[2,1024]{1,0:T(2,128)S(1)} %reshape.146.pair_ref, s32[1024,2]{1,0:T(8,128)S(1)} %bitcast.87, bf16[16,512,512]{2,1,0:T(8,128)(2,1)S(1)} %copy-done.1), custom_call_target="tpu_custom_call" | custom-call | tf_op jit(solution)/shard_map/beam/pallas_call | solution.py:289
  147.1 0.8 reshape.149
  (30 shorter events, 0.2 us)
Async XLA Ops:
  0.0 1.6 %copy-start.3 = (bf16[1,16,2,64,512]{4,3,2,1,0:T(8,128)(2,1)S(1)}, bf16[1,16,2,64,512]{4,3,2,1,0:T(8,128)(2,1)}, u32[]{:S(2)}) copy-start(bf16[1,16,2,64,512]{4,3,2,1,0:T(8,128)(2,1)} %param.5) | copy-start | bytes 6291460
  1.6 0.7 copy-start.7
  2.2 7.5 %copy-start.4 = (bf16[1,16,2,64,512]{4,3,2,1,0:T(8,128)(2,1)S(1)}, bf16[1,16,2,64,512]{4,3,2,1,0:T(8,128)(2,1)}, u32[]{:S(2)}) copy-start(bf16[1,16,2,64,512]{4,3,2,1,0:T(8,128)(2,1)} %param.5) | copy-start | bytes 6291460
  4.3 5.5 %collective-permute-start = (bf16[8,2,64,512]{3,2,1,0:T(8,128)(2,1)S(1)}, bf16[8,2,64,512]{3,2,1,0:T(8,128)(2,1)S(1)}, u32[]{:S(2)}, u32[]{:S(2)}) collective-permute-start(bf16[8,2,64,512]{3,2,1,0:T(8,128)(2,1)S(1)} %select.1), channel_id=1, source_target_pairs={{0,32},{32,0},{64,96},{96,64},{128,160},{160,128},{192,224},{224,1... | collective-permute-start | bytes 3145736 | tf_op jit(solution)/shard_map/ppermute | solution.py:308
  6.2 3.6 %collective-permute-start.1 = (f32[64,512]{1,0:T(8,128)}, f32[64,512]{1,0:T(8,128)S(1)}, u32[]{:S(2)}, u32[]{:S(2)}) collective-permute-start(f32[64,512]{1,0:T(8,128)} %bitcast.88), channel_id=1, source_target_pairs={{0,32},{32,0},{64,96},{96,64},{128,160},{160,128},{192,224},{224,1... | collective-permute-start | bytes 393224 | tf_op jit(solution)/shard_map/ppermute | solution.py:309
  9.8 0.9 copy-start.5
  10.7 0.7 copy-start.8
  14.1 33.9 %copy-start.2 = (f32[16,2,64,512]{3,2,1,0:T(8,128)}, f32[16,2,64,512]{3,2,1,0:T(8,128)S(1)}, u32[]{:S(2)}) copy-start(f32[16,2,64,512]{3,2,1,0:T(8,128)S(1)} %chip_sums.1) | copy-start | bytes 12582916
  14.1 5.1 %copy-start.6 = (f32[1,64,512]{2,1,0:T(8,128)S(1)}, f32[1,64,512]{2,1,0:T(8,128)}, u32[]{:S(2)}) copy-start(f32[1,64,512]{2,1,0:T(8,128)} %param.6) | copy-start | bytes 393220
  14.7 41.4 %copy-start.9 = (s32[16]{0:T(128)S(1)}, s32[16]{0:T(128)}, u32[]{:S(2)}) copy-start(s32[16]{0:T(128)} %offset_ref.3) | copy-start | bytes 196
  15.9 11.1 %collective-permute-start.9 = (f16[2,64,512]{2,1,0:T(8,128)(2,1)S(1)}, f16[2,64,512]{2,1,0:T(8,128)(2,1)S(1)}, u32[]{:S(2)}, u32[]{:S(2)}) collective-permute-start(f16[2,64,512]{2,1,0:T(8,128)(2,1)S(1)} %get-tuple-element.12), channel_id=1, source_target_pairs={{64,0},{96,32},{128,64},{160,96},{192,128},{224,160},{256,192},{28... | collective-permute-start | bytes 393224 | tf_op jit(solution)/shard_map/ppermute | solution.py:130
  27.0 26.1 %collective-permute-start.10 = (f16[2,64,512]{2,1,0:T(8,128)(2,1)S(1)}, f16[2,64,512]{2,1,0:T(8,128)(2,1)S(1)}, u32[]{:S(2)}, u32[]{:S(2)}) collective-permute-start(f16[2,64,512]{2,1,0:T(8,128)(2,1)S(1)} %fusion.5), channel_id=1, source_target_pairs={{64,0},{96,32},{128,64},{160,96},{192,128},{224,160},{256,192},{28... | collective-permute-start | bytes 393224 | tf_op jit(solution)/shard_map/ppermute | solution.py:130
  48.3 8.4 %collective-permute-start.13 = (f16[2,64,512]{2,1,0:T(8,128)(2,1)}, f16[2,64,512]{2,1,0:T(8,128)(2,1)S(1)}, u32[]{:S(2)}, u32[]{:S(2)}) collective-permute-start(f16[2,64,512]{2,1,0:T(8,128)(2,1)} %get-tuple-element.13), channel_id=1, source_target_pairs={{0,64},{32,96},{64,128},{96,160},{128,192},{160,224},{192,256},{22... | collective-permute-start | bytes 393224 | tf_op jit(solution)/shard_map/ppermute | solution.py:130
  54.1 8.6 %collective-permute-start.11 = (f16[2,64,512]{2,1,0:T(8,128)(2,1)S(1)}, f16[2,64,512]{2,1,0:T(8,128)(2,1)S(1)}, u32[]{:S(2)}, u32[]{:S(2)}) collective-permute-start(f16[2,64,512]{2,1,0:T(8,128)(2,1)S(1)} %fusion.7), channel_id=1, source_target_pairs={{64,0},{96,32},{128,64},{160,96},{192,128},{224,160},{256,192},{28... | collective-permute-start | bytes 393224 | tf_op jit(solution)/shard_map/ppermute | solution.py:130
  63.8 65.1 %copy-start.10 = (s32[2048]{0:T(1024)S(1)}, s32[2048]{0:T(1024)}, u32[]{:S(2)}) copy-start(s32[2048]{0:T(1024)} %param.9) | copy-start | bytes 24580
  63.8 12.1 %collective-permute-start.14 = (f16[2,64,512]{2,1,0:T(8,128)(2,1)S(1)}, f16[2,64,512]{2,1,0:T(8,128)(2,1)S(1)}, u32[]{:S(2)}, u32[]{:S(2)}) collective-permute-start(f16[2,64,512]{2,1,0:T(8,128)(2,1)S(1)} %get-tuple-element.9), channel_id=1, source_target_pairs={{0,64},{32,96},{64,128},{96,160},{128,192},{160,224},{192,256},{22... | collective-permute-start | bytes 393224 | tf_op jit(solution)/shard_map/ppermute | solution.py:130
  66.1 63.2 %copy-start.11 = (s32[2048]{0:T(1024)S(1)}, s32[2048]{0:T(1024)}, u32[]{:S(2)}) copy-start(s32[2048]{0:T(1024)} %param.8) | copy-start | bytes 24580
  66.1 14.0 %collective-permute-start.2 = (f16[2,64,512]{2,1,0:T(8,128)(2,1)}, f16[2,64,512]{2,1,0:T(8,128)(2,1)S(1)}, u32[]{:S(2)}, u32[]{:S(2)}) collective-permute-start(f16[2,64,512]{2,1,0:T(8,128)(2,1)} %get-tuple-element.15), channel_id=1, source_target_pairs={{0,64},{32,96},{64,128},{96,160},{128,192},{160,224},{192,256},{22... | collective-permute-start | bytes 393224 | tf_op jit(solution)/shard_map/ppermute | solution.py:130
  68.1 12.1 %collective-permute-start.6 = (f16[2,64,512]{2,1,0:T(8,128)(2,1)S(1)}, f16[2,64,512]{2,1,0:T(8,128)(2,1)S(1)}, u32[]{:S(2)}, u32[]{:S(2)}) collective-permute-start(f16[2,64,512]{2,1,0:T(8,128)(2,1)S(1)} %get-tuple-element.14), channel_id=1, source_target_pairs={{64,0},{96,32},{128,64},{160,96},{192,128},{224,160},{256,192},{28... | collective-permute-start | bytes 393224 | tf_op jit(solution)/shard_map/ppermute | solution.py:130
  72.0 8.2 %collective-permute-start.12 = (f16[2,64,512]{2,1,0:T(8,128)(2,1)S(1)}, f16[2,64,512]{2,1,0:T(8,128)(2,1)S(1)}, u32[]{:S(2)}, u32[]{:S(2)}) collective-permute-start(f16[2,64,512]{2,1,0:T(8,128)(2,1)S(1)} %get-tuple-element.8), channel_id=1, source_target_pairs={{64,0},{96,32},{128,64},{160,96},{192,128},{224,160},{256,192},{28... | collective-permute-start | bytes 393224 | tf_op jit(solution)/shard_map/ppermute | solution.py:130
  76.9 6.9 %collective-permute-start.15 = (f16[2,64,512]{2,1,0:T(8,128)(2,1)S(1)}, f16[2,64,512]{2,1,0:T(8,128)(2,1)S(1)}, u32[]{:S(2)}, u32[]{:S(2)}) collective-permute-start(f16[2,64,512]{2,1,0:T(8,128)(2,1)S(1)} %fusion.3), channel_id=1, source_target_pairs={{0,64},{32,96},{64,128},{96,160},{128,192},{160,224},{192,256},{22... | collective-permute-start | bytes 393224 | tf_op jit(solution)/shard_map/ppermute | solution.py:130
  85.0 6.9 %collective-permute-start.3 = (f16[2,64,512]{2,1,0:T(8,128)(2,1)S(1)}, f16[2,64,512]{2,1,0:T(8,128)(2,1)S(1)}, u32[]{:S(2)}, u32[]{:S(2)}) collective-permute-start(f16[2,64,512]{2,1,0:T(8,128)(2,1)S(1)} %get-tuple-element.7), channel_id=1, source_target_pairs={{0,64},{32,96},{64,128},{96,160},{128,192},{160,224},{192,256},{22... | collective-permute-start | bytes 393224 | tf_op jit(solution)/shard_map/ppermute | solution.py:130
  89.4 9.1 %collective-permute-start.7 = (f16[2,64,512]{2,1,0:T(8,128)(2,1)S(1)}, f16[2,64,512]{2,1,0:T(8,128)(2,1)S(1)}, u32[]{:S(2)}, u32[]{:S(2)}) collective-permute-start(f16[2,64,512]{2,1,0:T(8,128)(2,1)S(1)} %get-tuple-element.6), channel_id=1, source_target_pairs={{64,0},{96,32},{128,64},{160,96},{192,128},{224,160},{256,192},{28... | collective-permute-start | bytes 393224 | tf_op jit(solution)/shard_map/ppermute | solution.py:130
  92.9 8.1 %collective-permute-start.4 = (f16[2,64,512]{2,1,0:T(8,128)(2,1)S(1)}, f16[2,64,512]{2,1,0:T(8,128)(2,1)S(1)}, u32[]{:S(2)}, u32[]{:S(2)}) collective-permute-start(f16[2,64,512]{2,1,0:T(8,128)(2,1)S(1)} %fusion.19), channel_id=1, source_target_pairs={{0,64},{32,96},{64,128},{96,160},{128,192},{160,224},{192,256},{22... | collective-permute-start | bytes 393224 | tf_op jit(solution)/shard_map/ppermute | solution.py:130
  102.1 8.1 %collective-permute-start.5 = (f16[2,64,512]{2,1,0:T(8,128)(2,1)S(1)}, f16[2,64,512]{2,1,0:T(8,128)(2,1)S(1)}, u32[]{:S(2)}, u32[]{:S(2)}) collective-permute-start(f16[2,64,512]{2,1,0:T(8,128)(2,1)S(1)} %get-tuple-element.10), channel_id=1, source_target_pairs={{0,64},{32,96},{64,128},{96,160},{128,192},{160,224},{192,256},{22... | collective-permute-start | bytes 393224 | tf_op jit(solution)/shard_map/ppermute | solution.py:130
  107.7 8.1 %collective-permute-start.8 = (f16[2,64,512]{2,1,0:T(8,128)(2,1)S(1)}, f16[2,64,512]{2,1,0:T(8,128)(2,1)S(1)}, u32[]{:S(2)}, u32[]{:S(2)}) collective-permute-start(f16[2,64,512]{2,1,0:T(8,128)(2,1)S(1)} %get-tuple-element.11), channel_id=1, source_target_pairs={{64,0},{96,32},{128,64},{160,96},{192,128},{224,160},{256,192},{28... | collective-permute-start | bytes 393224 | tf_op jit(solution)/shard_map/ppermute | solution.py:130
  118.2 22.3 %all-to-all-start = ((bf16[32,32,128]{2,1,0:T(8,128)(2,1)}), bf16[32,32,128]{2,1,0:T(8,128)(2,1)S(1)}, u32[]{:S(2)}, u32[]{:S(2)}) async-start(bf16[32,32,128]{2,1,0:T(8,128)(2,1)} %pack.1), calls=%async_computation | async-start | bytes 524288 | tf_op jit(solution)/shard_map/all_to_all | solution.py:320
  134.8 3.3 %copy-start = (bf16[16,512,512]{2,1,0:T(8,128)(2,1)}, bf16[16,512,512]{2,1,0:T(8,128)(2,1)S(1)}, u32[]{:S(2)}) copy-start(bf16[16,512,512]{2,1,0:T(8,128)(2,1)S(1)} %table.1.table_ref) | copy-start | bytes 25165828
  140.5 3.4 %copy-start.1 = (bf16[16,512,512]{2,1,0:T(8,128)(2,1)S(1)}, bf16[16,512,512]{2,1,0:T(8,128)(2,1)}, u32[]{:S(2)}) copy-start(bf16[16,512,512]{2,1,0:T(8,128)(2,1)} %copy-done) | copy-start | bytes 25165828

commit v2 on v1

--- a/solution.py
+++ b/solution.py
@@ -23,6 +23,9 @@
 CHIPS = 8
 HELD = 8
 SCALE = 128.0
+N_Z = 8
+N_X = 4
+SWAP = [(d, d ^ 1) for d in range(DAYS)]
 
 F32 = jnp.float32
 BF16 = jnp.bfloat16
@@ -36,7 +39,7 @@
     return 2 * (offset >> 2) + jnp.clip((offset & 3) - 2 * core, 0, 2)
 
 
-def select_kernel(offset_ref, vis_ref, out_ref, sems):
+def select_kernel(offset_ref, weight_ref, vis_ref, out_ref, sems):
     day = lax.axis_index("day")
     other = 1 - (day & 1)
     offset = offset_ref[day]
@@ -51,86 +54,107 @@
             )
         )
         copies[-1].start()
+    weight = weight_ref[...]
+    high = weight.astype(BF16)
+    out_ref[HELD, 0] = high
+    out_ref[HELD, 1] = (weight - high.astype(F32)).astype(BF16)
     for copy in copies:
         copy.wait()
 
 
-def select(day_offset, visibility):
+def select(day_offset, day_weight, visibility):
     return pl.pallas_call(
         select_kernel,
-        in_specs=[pl.BlockSpec(memory_space=pltpu.SMEM), pl.BlockSpec(memory_space=pl.ANY)],
+        in_specs=[
+            pl.BlockSpec(memory_space=pltpu.SMEM),
+            pl.BlockSpec(memory_space=pltpu.VMEM),
+            pl.BlockSpec(memory_space=pltpu.HBM),
+        ],
         out_specs=pl.BlockSpec(memory_space=pltpu.VMEM),
-        out_shape=jax.ShapeDtypeStruct((HELD, 2, BASE_LOC, FREQ), BF16),
+        out_shape=jax.ShapeDtypeStruct((HELD + 1, 2, BASE_LOC, FREQ), BF16),
         scratch_shapes=[pltpu.SemaphoreType.DMA((HELD,))],
         compiler_params=pltpu.CompilerParams(vmem_limit_bytes=8 * MIB),
         name="select",
-    )(day_offset, visibility[0])
-
-
-def chip_kernel(offset_ref, vis_ref, weight_ref, other_vis_ref, other_weight_ref, out_ref):
+    )(day_offset, day_weight, visibility)
+
+
+SENDS = (
+    ((3, 0), (3, 1), (1, 0), (1, 1)),
+    ((5, 0), (5, 1), (7, 0), (7, 1)),
+    ((4, 0),),
+    ((4, 1),),
+    ((2, 0), (2, 1)),
+    ((6, 0), (6, 1)),
+    ((0, 0), (0, 1)),
+)
+
+
+def chip_kernel(offset_ref, vis_ref, weight_ref, other_ref, *out_refs):
     day = lax.axis_index("day")
     core = day & 1
     chip = day >> 1
     offset = offset_ref[day]
     first = bins_below(offset_ref[day ^ 1], core)
     weight = weight_ref[...] * SCALE
-    other_weight = other_weight_ref[...] * SCALE
-
-    def one_bin(at, _):
-        owned = 2 * ((chip + (at >> 1)) & (CHIPS - 1)) + (at & 1)
-        sample = 4 * (owned >> 1) + 2 * core + (owned & 1) - offset
-        valid = jnp.logical_and(sample >= 0, sample < SAMPLES)
-        held = jnp.logical_and(owned >= first, owned < first + HELD)
-        sample = jnp.clip(sample, 0, SAMPLES - 1)
-        own = weight * jnp.where(valid, 1.0, 0.0)
-        other = other_weight * jnp.where(held, 1.0, 0.0)
-        for x in range(2):
-            out_ref[at, x] = (
-                vis_ref[sample, x].astype(F32) * own
-                + other_vis_ref[owned & (HELD - 1), x].astype(F32) * other
-            )
-        return 0
-
-    lax.fori_loop(0, 2 * CHIPS, one_bin, 0)
-
-
-def chip_sums(day_offset, visibility, day_weight, other_vis, other_weight):
+    other_weight = (other_ref[HELD, 0].astype(F32) + other_ref[HELD, 1].astype(F32)) * SCALE
+    for out_ref, bins in zip(out_refs, SENDS):
+        for at, (distance, which) in enumerate(bins):
+            owned = 2 * ((chip + distance) & (CHIPS - 1)) + which
+            sample = 4 * (owned >> 1) + 2 * core + which - offset
+            valid = jnp.logical_and(sample >= 0, sample < SAMPLES)
+            held = jnp.logical_and(owned >= first, owned < first + HELD)
+            sample = jnp.clip(sample, 0, SAMPLES - 1)
+            own = weight * jnp.where(valid, 1.0, 0.0)
+            other = other_weight * jnp.where(held, 1.0, 0.0)
+            for x in range(2):
+                out_ref[at, x] = (
+                    vis_ref[sample, x].astype(F32) * own
+                    + other_ref[owned & (HELD - 1), x].astype(F32) * other
+                )
+
+
+def chip_sums(day_offset, visibility, day_weight, other):
     rows = 16
-    weight_spec = pl.BlockSpec((rows, FREQ), lambda i: (i, 0))
+    block = lambda count: pl.BlockSpec((count, 2, rows, FREQ), lambda i: (0, 0, i, 0))
     return pl.pallas_call(
         chip_kernel,
         grid=(BASE_LOC // rows,),
         in_specs=[
             pl.BlockSpec(memory_space=pltpu.SMEM),
-            pl.BlockSpec((SAMPLES, 2, rows, FREQ), lambda i: (0, 0, i, 0)),
-            weight_spec,
-            pl.BlockSpec((HELD, 2, rows, FREQ), lambda i: (0, 0, i, 0)),
-            weight_spec,
+            block(SAMPLES),
+            pl.BlockSpec((rows, FREQ), lambda i: (i, 0)),
+            block(HELD + 1),
         ],
-        out_specs=pl.BlockSpec((2 * CHIPS, 2, rows, FREQ), lambda i: (0, 0, i, 0)),
-        out_shape=jax.ShapeDtypeStruct((2 * CHIPS, 2, BASE_LOC, FREQ), F32),
+        out_specs=[block(len(bins)) for bins in SENDS],
+        out_shape=[
+            jax.ShapeDtypeStruct((len(bins), 2, BASE_LOC, FREQ), F32) for bins in SENDS
+        ],
         compiler_params=pltpu.CompilerParams(vmem_limit_bytes=16 * MIB),
         name="chip_sums",
-    )(day_offset, visibility[0], day_weight[0], other_vis, other_weight)
-
-
-def reduce_ring(chip_sum):
-    up = [(2 * y + c, 2 * ((y + 1) % CHIPS) + c) for y in range(CHIPS) for c in range(2)]
-    down = [(b, a) for a, b in up]
-    streams = [[up, 0, 4, 1], [down, 1, 4, -1], [up, 1, 3, 1], [down, 0, 3, -1]]
-    arrived = [None] * 4
-    for step in range(4):
-        for at, (pairs, which, hops, way) in enumerate(streams):
-            if step >= hops:
-                continue
-            distance = (way * (hops - step)) % CHIPS
-            own = chip_sum[2 * distance + which]
-            if step:
-                own = own + arrived[at].astype(F32)
-            arrived[at] = lax.ppermute(own.astype(F16), "day", pairs)
-    low = chip_sum[0] + arrived[0].astype(F32) + arrived[3].astype(F32)
-    high = chip_sum[1] + arrived[1].astype(F32) + arrived[2].astype(F32)
-    return low, high
+    )(day_offset, visibility, day_weight, other)
+
+
+def reduce_ring(sums):
+    def send(values, distance):
+        pairs = [
+            (2 * y + c, 2 * ((y + distance) % CHIPS) + c) for y in range(CHIPS) for c in range(2)
+        ]
+        return lax.ppermute(values.astype(F16), "day", pairs)
+
+    near_up, near_down = send(sums[0], 1), send(sums[1], -1)
+    far_up, far_down = send(sums[2], 2), send(sums[3], -2)
+    middle_up = sums[4] + near_up[:2].astype(F32)
+    middle_up = middle_up + jnp.pad(far_up.astype(F32), ((0, 1), (0, 0), (0, 0), (0, 0)))
+    middle_down = sums[5] + near_down[:2].astype(F32)
+    middle_down = middle_down + jnp.pad(far_down.astype(F32), ((1, 0), (0, 0), (0, 0), (0, 0)))
+    last_up, last_down = send(middle_up, 2), send(middle_down, -2)
+    return (
+        sums[6]
+        + near_up[2:].astype(F32)
+        + near_down[2:].astype(F32)
+        + last_up.astype(F32)
+        + last_down.astype(F32)
+    )
 
 
 def table_kernel(cos_a_ref, sin_a_ref, cos_b_ref, sin_b_ref, out_ref):
@@ -159,7 +183,7 @@
         grid=(BAND,),
         in_specs=[spec_a, spec_a, spec_b, spec_b],
         out_specs=pl.BlockSpec((1, NSEP, 2 * HALF), lambda f: (f, 0, 0)),
-        out_shape=jax.ShapeDtypeStruct((BAND, NSEP, 2 * HALF), BF16),
+        out_shape=pltpu.HBM((BAND, NSEP, 2 * HALF), BF16),
         compiler_params=pltpu.CompilerParams(vmem_limit_bytes=16 * MIB),
         cost_estimate=pl.CostEstimate(
             flops=6 * BAND * NSEP * HALF, bytes_accessed=4 * BAND * NSEP * HALF, transcendentals=0
@@ -168,12 +192,20 @@
     )(jnp.cos(phase_a), jnp.sin(phase_a), jnp.cos(phase_b), jnp.sin(phase_b))
 
 
-def inverse_total(day_offset, all_weights):
-    bins = lax.axis_index("day") * RA_DEV + jnp.arange(RA_DEV)
-    sample = bins[:, None] - day_offset[None, :]
-    valid = jnp.logical_and(sample >= 0, sample < SAMPLES).astype(F32)
-    total = jnp.sum(valid[:, :, None, None] * all_weights[None].astype(F32), axis=1)
-    return (1.0 / SCALE) / total
+def inverse_total(day_offset, day_weight):
+    day = lax.axis_index("day")
+    core = day & 1
+    same = [[2 * y + c for y in range(CHIPS)] for c in range(2)]
+    weights = lax.all_gather(day_weight, "day", axis=0, axis_index_groups=same)
+    offsets = jnp.where(core == 0, day_offset[0::2], day_offset[1::2])
+
+    def partial_total(owner):
+        sample = (owner * RA_DEV + jnp.arange(RA_DEV))[:, None] - offsets[None, :]
+        valid = jnp.logical_and(sample >= 0, sample < SAMPLES).astype(F32)
+        return jnp.sum(valid[:, :, None, None] * weights[None], axis=1)
+
+    other = lax.ppermute(partial_total(day ^ 1), "day", SWAP)
+    return (1.0 / SCALE) / (partial_total(day) + other)
 
 
 def pack_blocks(pieces, out_ref, rows):
@@ -196,7 +228,7 @@
             out_ref[tile * 8 + group, rows, :] = parts[group].astype(BF16)
 
 
-def pack_kernel(low_ref, high_ref, inverse_ref, out_ref):
+def pack_kernel(sum_ref, inverse_ref, table_ref, out_ref):
     half = BASE_LOC // 2
     for first in range(0, half, 16):
         for sub in range(0, 16, 8):
@@ -207,21 +239,21 @@
                     for hi in range(2):
                         rows_in = pl.ds(hi * half + first + sub, 8)
                         pieces.append(
-                            (low_ref, high_ref)[r][x, rows_in, :] * inverse_ref[r, rows_in, :]
+                            sum_ref[r, x, rows_in, :] * inverse_ref[r, rows_in, :]
                         )
             pack_blocks(pieces, out_ref, rows)
 
 
-def pack(low, high, inverse):
+def pack(summed, inverse, table):
     vmem = pl.BlockSpec(memory_space=pltpu.VMEM)
     return pl.pallas_call(
         pack_kernel,
-        in_specs=[vmem, vmem, vmem],
+        in_specs=[vmem, vmem, pl.BlockSpec(memory_space=pltpu.HBM)],
         out_specs=vmem,
         out_shape=jax.ShapeDtypeStruct((N_BL, BASE_LOC // 2, 128), BF16),
         compiler_params=pltpu.CompilerParams(vmem_limit_bytes=16 * MIB),
         name="pack",
-    )(low, high, inverse)
+    )(summed, inverse, table)
 
 
 def beam_kernel(block_ref, pair_ref, sep_ref, table_ref, out_ref, grid_ref):
@@ -304,26 +336,35 @@
 
 
 def day_stage(visibility, day_weight, day_offset):
-    swap = [(d, d ^ 1) for d in range(DAYS)]
-    other_vis = lax.ppermute(select(day_offset, visibility), "day", swap)
-    other_weight = lax.ppermute(day_weight[0], "day", swap)
-    all_weights = lax.all_gather(day_weight.astype(F16), "day", axis=0, tiled=True)
-    low, high = reduce_ring(
-        chip_sums(day_offset, visibility, day_weight, other_vis, other_weight)
-    )
-    return low, high, inverse_total(day_offset, all_weights)
-
-
-def beam_stage(low, high, inverse, pair_index, sep_index):
+    visibility, day_weight = visibility[0], day_weight[0]
+    inverse = inverse_total(day_offset, day_weight)
+    other = lax.ppermute(select(day_offset, day_weight, visibility), "day", SWAP)
+    summed = reduce_ring(chip_sums(day_offset, visibility, day_weight, other))
+    return summed, inverse
+
+
+def exchange(packed):
+    blocks = packed.reshape(N_Z, N_X, BASE_LOC // 2, 128)
+    along_z = [[z * N_X + x for z in range(N_Z)] for x in range(N_X)]
+    along_x = [[z * N_X + x for x in range(N_X)] for z in range(N_Z)]
+    blocks = lax.all_to_all(
+        blocks, "bl", split_axis=0, concat_axis=0, axis_index_groups=along_z, tiled=True
+    )
+    blocks = lax.all_to_all(
+        blocks, "bl", split_axis=1, concat_axis=1, axis_index_groups=along_x, tiled=True
+    )
+    return blocks.reshape(packed.shape)
+
+
+def beam_stage(summed, inverse, pair_index, sep_index):
     table = ns_table()
-    packed = pack(low, high, inverse)
-    block = lax.all_to_all(packed, "bl", split_axis=0, concat_axis=0, tiled=True)
+    block = exchange(pack(summed, inverse, table))
     return beam(block, pair_index, sep_index, table)
 
 
 def local(visibility, day_weight, day_offset, pair_index, sep_index):
-    low, high, inverse = day_stage(visibility, day_weight, day_offset)
-    result = beam_stage(low, high, inverse, pair_index, sep_index)
+    summed, inverse = day_stage(visibility, day_weight, day_offset)
+    result = beam_stage(summed, inverse, pair_index, sep_index)
     return result.reshape(BAND, RA_DEV, PAIRS, PIXELS)
 
 

time: 149 us -> 132 us (0.89)
  the two profiles are of different devices: /device:TPU:56 before, /device:TPU:1 now
where the time goes in v2:
time: 132 us
  starting transfers between devices  36.2 us (27%)
  waiting for transfers between devices  23.5 us (18%)
  blocking collectives  19.3 us (15%)
  Pallas kernels  18 us (14%)
  between operations  13.7 us (10%)
  local copies, waits for them, and re-layouts  12.2 us (9%)
  other arithmetic  8.74 us (7%)
    all_to_all x1, blocking collectives, exchange(): lax.all_to_all(blocks, 'bl', split_axis=0, concat_axis=0, axis_index_grou...  19.3 us
    ppermute x6, starting transfers between devices, send(): return lax.ppermute(values.astype(F16), 'day', pairs)  18.6 us
    ppermute x6, waiting for transfers between devices, send(): return lax.ppermute(values.astype(F16), 'day', pairs)  18 us
    unnamed x28, local copies, waits for them, and re-layouts  9.95 us
    ppermute x1, starting transfers between devices, day_stage(): lax.ppermute(select(day_offset, day_weight, visibility), 'day', SWAP)  8.79 us
    pallas_call x1, Pallas kernels, ns_table(): pl.pallas_call(table_kernel, grid=(BAND,), in_specs=[spec_a, spec_a, spec...  7.79 us
    all_to_all x1, waiting for transfers between devices, exchange(): lax.all_to_all(blocks, 'bl', split_axis=1, concat_axis=1, axis_index_grou...  5 us
    ppermute x1, starting transfers between devices, inverse_total(): other = lax.ppermute(partial_total(day ^ 1), 'day', SWAP)  4.83 us
  transfers between devices with their start and end apart: 10, of which 5 were waited for; matrix products, arithmetic and copies ran while one was open for 7% of the time, Pallas kernels for 8%

profile of v2, /device:TPU:1, one launch (start us, length us, event | category | flops | bytes accessed | tf_op | source)
XLA Modules:
  0.0 131.7 jit_solution(16784849745204849952)
XLA Ops:
  6.5 0.0 all-gather.2.cloned.1.call-start
  6.5 1.6 %copy-done.2 = bf16[1,16,2,64,512]{4,3,2,1,0:T(8,128)(2,1)S(1)} copy-done((bf16[1,16,2,64,512]{4,3,2,1,0:T(8,128)(2,1)S(1)}, bf16[1,16,2,64,512]{4,3,2,1,0:T(8,128)(2,1)}, u32[]{:S(2)}) %copy-start.2) | copy-done | bytes 2097176
  8.1 0.9 copy-done.4
  9.0 0.7 copy-done.10
  9.7 3.1 %select.3 = bf16[9,2,64,512]{3,2,1,0:T(8,128)(2,1)} custom-call(s32[16]{0:T(128)S(1)} %copy-done.10, f32[64,512]{1,0:T(8,128)S(1)} %bitcast.10, bf16[16,2,64,512]{3,2,1,0:T(8,128)(2,1)S(1)} %bitcast.7), custom_call_target="tpu_custom_call" | custom-call | tf_op jit(solution)/shard_map/select/pallas_call | solution.py:66
  12.8 8.8 %collective-permute-start = (bf16[9,2,64,512]{3,2,1,0:T(8,128)(2,1)}, bf16[9,2,64,512]{3,2,1,0:T(8,128)(2,1)}, u32[]{:S(2)}, u32[]{:S(2)}) collective-permute-start(bf16[9,2,64,512]{3,2,1,0:T(8,128)(2,1)} %select.3), channel_id=1, source_target_pairs={{0,32},{32,0},{64,96},{96,64},{128,160},{160,128},{192,224},{224,1... | collective-permute-start | bytes 3538952 | tf_op jit(solution)/shard_map/ppermute | solution.py:341
  21.6 0.0 all-gather.2.cloned.1.call-update
  21.6 0.0 copy-done.11
  21.6 0.1 slice.22
  21.7 0.1 slice.23
  21.9 0.1 broadcast_multiply_fusion.1
  21.9 0.1 broadcast_multiply_fusion
  22.0 1.9 %multiply_sine_fusion = (f32[16,32,256]{2,1,0:T(8,128)S(1)}, f32[16,32,256]{2,1,0:T(8,128)S(1)}) fusion(f32[256]{0:T(256)S(1)} %multiply_add_fusion, f32[16,32]{1,0:T(8,128)S(1)} %broadcast_multiply_fusion.1), kind=kLoop, calls=%fused_computation.2 | loop fusion | flops 131072 | bytes 1051648 | tf_op jit(solution)/shard_map/sin | solution.py:192
  23.9 0.5 collective-permute-done.other_ref
  24.4 0.0 copy-done.3
  24.4 0.0 copy-done.5
  24.4 3.2 %chip_sums.1 = (f32[4,2,64,512]{3,2,1,0:T(8,128)S(1)}, f32[4,2,64,512]{3,2,1,0:T(8,128)S(1)}, f32[1,2,64,512]{3,2,1,0:T(8,128)S(1)}, f32[1,2,64,512]{3,2,1,0:T(8...) custom-call(s32[16]{0:T(128)S(1)} %copy-done.11, ...), custom_call_target="tpu_custom_call" | custom-call | tf_op jit(solution)/shard_map/chip_sums/pallas_call | solution.py:119
  27.6 0.0 copy-start.6
  27.6 0.0 copy-start.7
  27.6 0.0 copy-start.8
  27.6 0.1 convert_element_type.86
  27.7 1.9 %collective-permute-start.1 = (f16[4,2,64,512]{3,2,1,0:T(8,128)(2,1)S(1)}, f16[4,2,64,512]{3,2,1,0:T(8,128)(2,1)S(1)}, u32[]{:S(2)}, u32[]{:S(2)}) collective-permute-start(f16[4,2,64,512]{3,2,1,0:T(8,128)(2,1)S(1)} %convert_element_type.86), channel_id=1, source_target_pairs={{0,64},{32,96},{64,128},{96,160},{128,192},{160,224},{192,256},{22... | collective-permute-start | bytes 1572872 | tf_op jit(solution)/shard_map/ppermute | solution.py:142
  29.6 1.0 multiply_sine_fusion.1
  30.6 1.9 %collective-permute-start.3 = (f16[1,2,64,512]{3,2,1,0:T(8,128)(2,1)S(1)}, f16[1,2,64,512]{3,2,1,0:T(8,128)(2,1)}, u32[]{:S(2)}, u32[]{:S(2)}) collective-permute-start(f16[1,2,64,512]{3,2,1,0:T(8,128)(2,1)S(1)} %convert_element_type.91), channel_id=1, source_target_pairs={{0,128},{32,160},{64,192},{96,224},{128,256},{160,288},{192,320},{... | collective-permute-start | bytes 393224 | tf_op jit(solution)/shard_map/ppermute | solution.py:142
  32.6 0.1 convert_element_type.88
  32.7 0.0 copy-done.6
  32.7 4.6 %collective-permute-start.2 = (f16[4,2,64,512]{3,2,1,0:T(8,128)(2,1)S(1)}, f16[4,2,64,512]{3,2,1,0:T(8,128)(2,1)}, u32[]{:S(2)}, u32[]{:S(2)}) collective-permute-start(f16[4,2,64,512]{3,2,1,0:T(8,128)(2,1)S(1)} %convert_element_type.88), channel_id=1, source_target_pairs={{0,448},{32,480},{64,0},{96,32},{128,64},{160,96},{192,128},{224,1... | collective-permute-start | bytes 1572872 | tf_op jit(solution)/shard_map/ppermute | solution.py:142
  37.3 0.0 copy-done.7
  37.3 0.0 copy-done.8
  37.3 4.3 %collective-permute-start.5 = (f16[1,2,64,512]{3,2,1,0:T(8,128)(2,1)S(1)}, f16[1,2,64,512]{3,2,1,0:T(8,128)(2,1)S(1)}, u32[]{:S(2)}, u32[]{:S(2)}) collective-permute-start(f16[1,2,64,512]{3,2,1,0:T(8,128)(2,1)S(1)} %convert_element_type.95), channel_id=1, source_target_pairs={{0,384},{32,416},{64,448},{96,480},{128,0},{160,32},{192,64},{224,... | collective-permute-start | bytes 393224 | tf_op jit(solution)/shard_map/ppermute | solution.py:142
  41.6 6.4 %collective-permute-done.3 = f16[1,2,64,512]{3,2,1,0:T(8,128)(2,1)} collective-permute-done((f16[1,2,64,512]{3,2,1,0:T(8,128)(2,1)S(1)}, f16[1,2,64,512]{3,2,1,0:T(8,128)(2,1)}, u32[]{:S(2)}, u32[]{:S(2)}) %collective-permute-start.3) | collective-permute-done | bytes 131104 | tf_op jit(solution)/shard_map/ppermute | solution.py:142
  48.0 3.8 %collective-permute-done.1 = f16[4,2,64,512]{3,2,1,0:T(8,128)(2,1)S(1)} collective-permute-done((f16[4,2,64,512]{3,2,1,0:T(8,128)(2,1)S(1)}, f16[4,2,64,512]{3,2,1,0:T(8,128)(2,1)S(1)}, u32[]{:S(2)}, u32[]{:S(2)}) %collective-permute-start.1) | collective-permute-done | bytes 524320 | tf_op jit(solution)/shard_map/ppermute | solution.py:142
  51.8 1.2 add_convert_fusion.1
  53.0 1.9 %collective-permute-start.4 = (f16[2,2,64,512]{3,2,1,0:T(8,128)(2,1)S(1)}, f16[2,2,64,512]{3,2,1,0:T(8,128)(2,1)}, u32[]{:S(2)}, u32[]{:S(2)}) collective-permute-start(f16[2,2,64,512]{3,2,1,0:T(8,128)(2,1)S(1)} %add_convert_fusion.1), channel_id=1, source_target_pairs={{0,128},{32,160},{64,192},{96,224},{128,256},{160,288},{192,320},{... | collective-permute-start | bytes 786440 | tf_op jit(solution)/shard_map/ppermute | solution.py:142
  54.9 7.7 %collective-permute-done.5 = f16[1,2,64,512]{3,2,1,0:T(8,128)(2,1)S(1)} collective-permute-done((f16[1,2,64,512]{3,2,1,0:T(8,128)(2,1)S(1)}, f16[1,2,64,512]{3,2,1,0:T(8,128)(2,1)S(1)}, u32[]{:S(2)}, u32[]{:S(2)}) %collective-permute-start.5) | collective-permute-done | bytes 131104 | tf_op jit(solution)/shard_map/ppermute | solution.py:142
  62.7 0.0 collective-permute-done.2
  62.7 1.2 add_convert_fusion
  63.9 4.0 %collective-permute-start.6 = (f16[2,2,64,512]{3,2,1,0:T(8,128)(2,1)S(1)}, f16[2,2,64,512]{3,2,1,0:T(8,128)(2,1)}, u32[]{:S(2)}, u32[]{:S(2)}) collective-permute-start(f16[2,2,64,512]{3,2,1,0:T(8,128)(2,1)S(1)} %add_convert_fusion), channel_id=1, source_target_pairs={{0,384},{32,416},{64,448},{96,480},{128,0},{160,32},{192,64},{224,... | collective-permute-start | bytes 786440 | tf_op jit(solution)/shard_map/ppermute | solution.py:142
  67.9 0.1 and_convert_fusion.1
  68.0 7.8 %table.1.table_ref = bf16[16,512,512]{2,1,0:T(8,128)(2,1)} custom-call(f32[16,32,256]{2,1,0:T(8,128)S(1)} %get-tuple-element.24.cos_a_ref, f32[16,32,256]{2,1,0:T(8,128)S(1)} %get-tuple-element.23.sin_a_ref, f32[16,16,256]{2,1,0:T(8,128)S(1)} %get-tuple-element.22.cos_b_ref, f32[16,16,256]{2,1,0:T(8,128)S(1)} %get-tuple-element.21.sin_b_ref), custom_call_target="tpu_custom_call" | custom-call | flops 12582912 | bytes 8388608 | tf_op jit(solution)/shard_map/table/pallas_call | solution.py:181
  75.8 1.6 %multiply_reduce_fusion = (f32[2,64,512]{2,1,0:T(8,128)S(1)}, f32[2,64,512]{2,1,0:T(8,128)S(1)}) fusion(f32[2,8]{1,0:T(2,128)S(1)} %get-tuple-element.26, f32[8,64,512]{2,1,0:T(8,128)} %all-gather.2.cloned.1.call-done, f32[2,8]{1,0:T(2,128)S(1)} %get-tuple-element.25), kind=kLoop, calls=%fused_computation | loop fusion | flops 1966080 | bytes 1572992 | tf_op jit(solution)/shard_map/reduce_sum | solution.py:205
  77.5 4.8 %collective-permute-start.7 = (f32[2,64,512]{2,1,0:T(8,128)S(1)}, f32[2,64,512]{2,1,0:T(8,128)S(1)}, u32[]{:S(2)}, u32[]{:S(2)}) collective-permute-start(f32[2,64,512]{2,1,0:T(8,128)S(1)} %get-tuple-element.19), channel_id=1, source_target_pairs={{0,32},{32,0},{64,96},{96,64},{128,160},{160,128},{192,224},{224,1... | collective-permute-start | bytes 786440 | tf_op jit(solution)/shard_map/ppermute | solution.py:207
  82.3 0.0 collective-permute-done.4
  82.3 0.0 collective-permute-done.6
  82.3 0.0 copy-done.9
  82.3 1.3 convert_add_fusion.sum_ref
  83.6 0.0 collective-permute-done.7
  83.6 0.1 add_divide_fusion.inverse_ref
  83.7 0.0 copy-start
  83.7 3.4 %copy-done = bf16[16,512,512]{2,1,0:T(8,128)(2,1)S(1)} copy-done((bf16[16,512,512]{2,1,0:T(8,128)(2,1)S(1)}, bf16[16,512,512]{2,1,0:T(8,128)(2,1)}, u32[]{:S(2)}) %copy-start) | copy-done | bytes 8388632
  87.1 0.7 pack.1
  87.8 0.0 copy-start.13
  87.8 19.3 %all_to_all.10 = bf16[8,4,32,128]{3,2,1,0:T(8,128)(2,1)S(1)} all-to-all(bf16[8,4,32,128]{3,2,1,0:T(8,128)(2,1)S(1)} %bitcast.13), channel_id=1, replica_groups={{0,4,8,12,16,20,24,28},{1,5,9,13,17,21,25,29},{2,6,10,14,18,22,26,30},{..., dimensions={0} | all-to-all | bytes 524288 | tf_op jit(solution)/shard_map/all_to_all | solution.py:350
  107.1 0.7 copy.16
  107.9 4.0 %all-to-all-start.1 = ((bf16[8,4,32,128]{3,2,0,1:T(8,128)(2,1)}), bf16[8,4,32,128]{3,2,0,1:T(8,128)(2,1)S(1)}, u32[]{:S(2)}, u32[]{:S(2)}) async-start(bf16[8,4,32,128]{3,2,0,1:T(8,128)(2,1)} %copy.16), calls=%async_computation.1 | async-start | bytes 524288 | tf_op jit(solution)/shard_map/all_to_all | solution.py:353
  111.8 0.0 copy-done.12
  111.8 0.1 reshape.182
  111.9 0.3 copy.19
  112.2 0.1 reshape.180
  112.3 0.1 reshape.181.pair_ref
  112.4 5.0 %all-to-all-done.1 = bf16[8,4,32,128]{3,2,0,1:T(8,128)(2,1)S(1)} async-done(((bf16[8,4,32,128]{3,2,0,1:T(8,128)(2,1)}), bf16[8,4,32,128]{3,2,0,1:T(8,128)(2,1)S(1)}, u32[]{:S(2)}, u32[]{:S(2)}) %all-to-all-start.1) | async-done | bytes 262176 | tf_op jit(solution)/shard_map/all_to_all | solution.py:353
  117.4 3.4 %copy-done.1 = bf16[16,512,512]{2,1,0:T(8,128)(2,1)S(1)} copy-done((bf16[16,512,512]{2,1,0:T(8,128)(2,1)S(1)}, bf16[16,512,512]{2,1,0:T(8,128)(2,1)}, u32[]{:S(2)}) %copy-start.1) | copy-done | bytes 8388632
  120.8 3.3 %beam.1 = f32[16,8,512]{2,1,0:T(8,128)S(1)} custom-call(bf16[32,32,128]{2,1,0:T(8,128)(2,1)S(1)} %bitcast.12, s32[2,1024]{1,0:T(2,128)S(1)} %reshape.181.pair_ref, s32[1024,2]{1,0:T(8,128)S(1)} %bitcast.9, bf16[16,512,512]{2,1,0:T(8,128)(2,1)S(1)} %copy-done.1), custom_call_target="tpu_custom_call" | custom-call | tf_op jit(solution)/shard_map/beam/pallas_call | solution.py:321
  124.1 0.8 reshape.184
  (21 shorter events, 0.1 us)
Async XLA Ops:
  6.5 15.1 %copy-start.11 = (s32[16]{0:T(128)S(1)}, s32[16]{0:T(128)}, u32[]{:S(2)}) copy-start(s32[16]{0:T(128)} %offset_ref.3) | copy-start | bytes 196
  6.5 69.3 %all-gather.2.cloned.1.call-start = ((), (), s32[]{:S(2)}) async-start(), calls=%async_computation.2 | async-start | bytes 1179648 | tf_op jit(solution)/shard_map/all_gather | solution.py:199
  6.5 1.6 %copy-start.2 = (bf16[1,16,2,64,512]{4,3,2,1,0:T(8,128)(2,1)S(1)}, bf16[1,16,2,64,512]{4,3,2,1,0:T(8,128)(2,1)}, u32[]{:S(2)}) copy-start(bf16[1,16,2,64,512]{4,3,2,1,0:T(8,128)(2,1)} %param.5) | copy-start | bytes 6291460
  8.1 0.9 copy-start.4
  9.0 0.7 copy-start.10
  9.7 14.7 %copy-start.3 = (bf16[1,16,2,64,512]{4,3,2,1,0:T(8,128)(2,1)S(1)}, bf16[1,16,2,64,512]{4,3,2,1,0:T(8,128)(2,1)}, u32[]{:S(2)}) copy-start(bf16[1,16,2,64,512]{4,3,2,1,0:T(8,128)(2,1)} %param.5) | copy-start | bytes 6291460
  9.7 14.7 %copy-start.5 = (f32[1,64,512]{2,1,0:T(8,128)S(1)}, f32[1,64,512]{2,1,0:T(8,128)}, u32[]{:S(2)}) copy-start(f32[1,64,512]{2,1,0:T(8,128)} %param.6) | copy-start | bytes 393220
  12.8 11.6 %collective-permute-start = (bf16[9,2,64,512]{3,2,1,0:T(8,128)(2,1)}, bf16[9,2,64,512]{3,2,1,0:T(8,128)(2,1)}, u32[]{:S(2)}, u32[]{:S(2)}) collective-permute-start(bf16[9,2,64,512]{3,2,1,0:T(8,128)(2,1)} %select.3), channel_id=1, source_target_pairs={{0,32},{32,0},{64,96},{96,64},{128,160},{160,128},{192,224},{224,1... | collective-permute-start | bytes 3538952 | tf_op jit(solution)/shard_map/ppermute | solution.py:341
  27.6 5.1 %copy-start.6 = (f32[2,2,64,512]{3,2,1,0:T(8,128)}, f32[2,2,64,512]{3,2,1,0:T(8,128)S(1)}, u32[]{:S(2)}) copy-start(f32[2,2,64,512]{3,2,1,0:T(8,128)S(1)} %get-tuple-element.17) | copy-start | bytes 1572868
  27.6 9.7 %copy-start.7 = (f32[2,2,64,512]{3,2,1,0:T(8,128)}, f32[2,2,64,512]{3,2,1,0:T(8,128)S(1)}, u32[]{:S(2)}) copy-start(f32[2,2,64,512]{3,2,1,0:T(8,128)S(1)} %get-tuple-element.15) | copy-start | bytes 1572868
  27.6 9.7 %copy-start.8 = (f32[2,2,64,512]{3,2,1,0:T(8,128)}, f32[2,2,64,512]{3,2,1,0:T(8,128)S(1)}, u32[]{:S(2)}) copy-start(f32[2,2,64,512]{3,2,1,0:T(8,128)S(1)} %get-tuple-element.12) | copy-start | bytes 1572868
  27.7 24.1 %collective-permute-start.1 = (f16[4,2,64,512]{3,2,1,0:T(8,128)(2,1)S(1)}, f16[4,2,64,512]{3,2,1,0:T(8,128)(2,1)S(1)}, u32[]{:S(2)}, u32[]{:S(2)}) collective-permute-start(f16[4,2,64,512]{3,2,1,0:T(8,128)(2,1)S(1)} %convert_element_type.86), channel_id=1, source_target_pairs={{0,64},{32,96},{64,128},{96,160},{128,192},{160,224},{192,256},{22... | collective-permute-start | bytes 1572872 | tf_op jit(solution)/shard_map/ppermute | solution.py:142
  30.6 17.4 %collective-permute-start.3 = (f16[1,2,64,512]{3,2,1,0:T(8,128)(2,1)S(1)}, f16[1,2,64,512]{3,2,1,0:T(8,128)(2,1)}, u32[]{:S(2)}, u32[]{:S(2)}) collective-permute-start(f16[1,2,64,512]{3,2,1,0:T(8,128)(2,1)S(1)} %convert_element_type.91), channel_id=1, source_target_pairs={{0,128},{32,160},{64,192},{96,224},{128,256},{160,288},{192,320},{... | collective-permute-start | bytes 393224 | tf_op jit(solution)/shard_map/ppermute | solution.py:142
  32.7 30.0 %collective-permute-start.2 = (f16[4,2,64,512]{3,2,1,0:T(8,128)(2,1)S(1)}, f16[4,2,64,512]{3,2,1,0:T(8,128)(2,1)}, u32[]{:S(2)}, u32[]{:S(2)}) collective-permute-start(f16[4,2,64,512]{3,2,1,0:T(8,128)(2,1)S(1)} %convert_element_type.88), channel_id=1, source_target_pairs={{0,448},{32,480},{64,0},{96,32},{128,64},{160,96},{192,128},{224,1... | collective-permute-start | bytes 1572872 | tf_op jit(solution)/shard_map/ppermute | solution.py:142
  37.3 25.3 %collective-permute-start.5 = (f16[1,2,64,512]{3,2,1,0:T(8,128)(2,1)S(1)}, f16[1,2,64,512]{3,2,1,0:T(8,128)(2,1)S(1)}, u32[]{:S(2)}, u32[]{:S(2)}) collective-permute-start(f16[1,2,64,512]{3,2,1,0:T(8,128)(2,1)S(1)} %convert_element_type.95), channel_id=1, source_target_pairs={{0,384},{32,416},{64,448},{96,480},{128,0},{160,32},{192,64},{224,... | collective-permute-start | bytes 393224 | tf_op jit(solution)/shard_map/ppermute | solution.py:142
  53.0 29.3 %collective-permute-start.4 = (f16[2,2,64,512]{3,2,1,0:T(8,128)(2,1)S(1)}, f16[2,2,64,512]{3,2,1,0:T(8,128)(2,1)}, u32[]{:S(2)}, u32[]{:S(2)}) collective-permute-start(f16[2,2,64,512]{3,2,1,0:T(8,128)(2,1)S(1)} %add_convert_fusion.1), channel_id=1, source_target_pairs={{0,128},{32,160},{64,192},{96,224},{128,256},{160,288},{192,320},{... | collective-permute-start | bytes 786440 | tf_op jit(solution)/shard_map/ppermute | solution.py:142
  63.9 18.4 %collective-permute-start.6 = (f16[2,2,64,512]{3,2,1,0:T(8,128)(2,1)S(1)}, f16[2,2,64,512]{3,2,1,0:T(8,128)(2,1)}, u32[]{:S(2)}, u32[]{:S(2)}) collective-permute-start(f16[2,2,64,512]{3,2,1,0:T(8,128)(2,1)S(1)} %add_convert_fusion), channel_id=1, source_target_pairs={{0,384},{32,416},{64,448},{96,480},{128,0},{160,32},{192,64},{224,... | collective-permute-start | bytes 786440 | tf_op jit(solution)/shard_map/ppermute | solution.py:142
  68.0 14.3 %copy-start.9 = (f32[2,2,64,512]{3,2,1,0:T(8,128)S(1)}, f32[2,2,64,512]{3,2,1,0:T(8,128)}, u32[]{:S(2)}) copy-start(f32[2,2,64,512]{3,2,1,0:T(8,128)} %copy-done.8) | copy-start | bytes 1572868
  77.5 6.2 %collective-permute-start.7 = (f32[2,64,512]{2,1,0:T(8,128)S(1)}, f32[2,64,512]{2,1,0:T(8,128)S(1)}, u32[]{:S(2)}, u32[]{:S(2)}) collective-permute-start(f32[2,64,512]{2,1,0:T(8,128)S(1)} %get-tuple-element.19), channel_id=1, source_target_pairs={{0,32},{32,0},{64,96},{96,64},{128,160},{160,128},{192,224},{224,1... | collective-permute-start | bytes 786440 | tf_op jit(solution)/shard_map/ppermute | solution.py:207
  83.7 3.4 %copy-start = (bf16[16,512,512]{2,1,0:T(8,128)(2,1)S(1)}, bf16[16,512,512]{2,1,0:T(8,128)(2,1)}, u32[]{:S(2)}) copy-start(bf16[16,512,512]{2,1,0:T(8,128)(2,1)} %table.1.table_ref) | copy-start | bytes 25165828
  87.1 24.7 %copy-start.12 = (s32[2048]{0:T(1024)S(1)}, s32[2048]{0:T(1024)}, u32[]{:S(2)}) copy-start(s32[2048]{0:T(1024)} %param.9) | copy-start | bytes 24580
  87.8 24.4 %copy-start.13 = (s32[2048]{0:T(1024)S(1)}, s32[2048]{0:T(1024)}, u32[]{:S(2)}) copy-start(s32[2048]{0:T(1024)} %param.8) | copy-start | bytes 24580
  107.9 9.5 %all-to-all-start.1 = ((bf16[8,4,32,128]{3,2,0,1:T(8,128)(2,1)}), bf16[8,4,32,128]{3,2,0,1:T(8,128)(2,1)S(1)}, u32[]{:S(2)}, u32[]{:S(2)}) async-start(bf16[8,4,32,128]{3,2,0,1:T(8,128)(2,1)} %copy.16), calls=%async_computation.1 | async-start | bytes 524288 | tf_op jit(solution)/shard_map/all_to_all | solution.py:353
  117.4 3.4 %copy-start.1 = (bf16[16,512,512]{2,1,0:T(8,128)(2,1)S(1)}, bf16[16,512,512]{2,1,0:T(8,128)(2,1)}, u32[]{:S(2)}) copy-start(bf16[16,512,512]{2,1,0:T(8,128)(2,1)} %table.1.table_ref) | copy-start | bytes 25165828
Sparse Core Ops, SparseCore 0:
  21.7 44.1 all-gather.1
